TPU v7x, 32 devices: a whole 2x2x4 slice. The times are simulated.
32 devices in a mesh: tables: 8 (over z, x), heads: 4 (over y, core).
Axes of the slice: x: 2, y: 2, z: 4, core: 2. Of those that a mesh axis runs over, the one named last changes fastest.
Arguments:
- ctx_feat: bfloat16 [8, 2048, 100], P('tables', 'heads'), may hold values from -6 to 6
- qry_feat: bfloat16 [8, 704, 100], P('tables', 'heads'), may hold values from -6 to 6
- counts: int32 [8], P('tables'), may hold values from 64 to 2048, as said below
- ctx_bins: int32 [8, 2048], P('tables', 'heads'), may hold values from 0 to 63
- qry_bins: int32 [8, 704], P('tables', 'heads'), may hold values from 0 to 63
- query_mask: int32 [8, 704], P('tables', 'heads'), may hold values from 0 to 1
- w_embed: float32 [100, 768], replicated, may hold values from -0.625 to 0.625
- w_bins: float32 [64, 768], replicated, may hold values from -6 to 6
- norm_gains: float32 [3, 768], replicated, may hold values from 0.5 to 1.5
- w_qkv: float32 [3, 768, 768], P(None, None, 'heads'), may hold values from -0.21875 to 0.21875
- w_out: float32 [768, 768], P('heads')
- w_up: float32 [768, 3072], P(None, 'heads')
- w_down: float32 [3072, 768], P('heads')
- w_head: float32 [768, 64], replicated, may hold values from -0.21875 to 0.21875
- m_embed: float32 [100, 768], replicated, may hold values from -4.7683716e-06 to 4.7683716e-06
- m_bins: float32 [64, 768], replicated, may hold values from -1.9073486e-06 to 1.9073486e-06
- m_gains: float32 [3, 768], replicated, may hold values from -2.2888184e-05 to 2.2888184e-05
- m_qkv: float32 [3, 768, 768], P(None, None, 'heads'), may hold values from -4.7683716e-06 to 4.7683716e-06
- m_out: float32 [768, 768], P('heads'), may hold values from -2.3841858e-07 to 2.3841858e-07
- m_up: float32 [768, 3072], P(None, 'heads'), may hold values from -9.536743e-07 to 9.536743e-07
- m_down: float32 [3072, 768], P('heads'), may hold values from -4.7683716e-06 to 4.7683716e-06
- m_head: float32 [768, 64], replicated, may hold values from -4.7683716e-06 to 4.7683716e-06
- v_embed: float32 [100, 768], replicated, may hold values from 2.756607e-12 to 1.1026428e-11
- v_bins: float32 [64, 768], replicated, may hold values from 4.4105713e-13 to 1.7642285e-12
- v_gains: float32 [3, 768], replicated, may hold values from 6.891518e-11 to 2.7566072e-10
- v_qkv: float32 [3, 768, 768], P(None, None, 'heads'), may hold values from 2.756607e-12 to 1.1026428e-11
- v_out: float32 [768, 768], P('heads'), may hold values from 6.8915177e-15 to 2.756607e-14
- v_up: float32 [768, 3072], P(None, 'heads'), may hold values from 1.1026428e-13 to 4.4105713e-13
- v_down: float32 [3072, 768], P('heads'), may hold values from 2.756607e-12 to 1.1026428e-11
- v_head: float32 [768, 64], replicated, may hold values from 2.756607e-12 to 1.1026428e-11
Outputs:
- embed_new: float32 [100, 768], replicated
- bins_new: float32 [64, 768], replicated
- gains_new: float32 [3, 768], replicated
- qkv_new: float32 [3, 768, 768], P(None, None, 'heads')
- out_new: float32 [768, 768], P('heads')
- up_new: float32 [768, 3072], P(None, 'heads')
- down_new: float32 [3072, 768], P('heads')
- head_new: float32 [768, 64], replicated
- embed_first: float32 [100, 768], replicated
- bins_first: float32 [64, 768], replicated
- gains_first: float32 [3, 768], replicated
- qkv_first: float32 [3, 768, 768], P(None, None, 'heads')
- out_first: float32 [768, 768], P('heads')
- up_first: float32 [768, 3072], P(None, 'heads')
- down_first: float32 [3072, 768], P('heads')
- head_first: float32 [768, 64], replicated
- embed_second: float32 [100, 768], replicated
- bins_second: float32 [64, 768], replicated
- gains_second: float32 [3, 768], replicated
- qkv_second: float32 [3, 768, 768], P(None, None, 'heads')
- out_second: float32 [768, 768], P('heads')
- up_second: float32 [768, 3072], P(None, 'heads')
- down_second: float32 [3072, 768], P('heads')
- head_second: float32 [768, 64], replicated
- loss_sum: float32 [], replicated
- query_count: float32 [], replicated
- grad_norm: float32 [], replicated
Inputs may be any that keep to these rules, and one draw needn't show every extreme that they name: `counts`: one table, drawn from the seed, has all 2048 slots live.
All inputs are finite; a program needn't handle non-finite values.
Results may differ from a plain program's by a relative error of at most 0.013.
The roundings to bfloat16 on the way count: a program that leaves them out, or rounds other values in their place, can miss the bound.
Values may be sent and summed in bfloat16 or wider, within the bound.
A program may use at most 256 MiB of HBM per device.

v0:
```python
import jax
import jax.numpy as jnp
from jax import lax
from jax.sharding import PartitionSpec as P

HD = 64
BINS = 64
STEP = 10


NORM_EPS = 1e-05
ADAM_EPS = 1e-08
RATE = 0.05
RATE_WIDE = 1.0
BETA_ONE = 0.9
BETA_TWO = 0.95
DECAY = 0.1
CLIP_NORM = 0.02
MASKED = -1e30
FLOAT = jnp.float32
HALF = jnp.bfloat16


def product(left, right):
    return jnp.dot(left, right, preferred_element_type=FLOAT)


def normalize(hidden, gain_row):
    center = hidden - jnp.mean(hidden, axis=-1, keepdims=True)
    spread = jnp.mean(center * center, axis=-1, keepdims=True)
    return center * lax.rsqrt(spread + NORM_EPS) * gain_row


def norm_back(hidden, gain_row, upstream):
    _, pullback = jax.vjp(normalize, hidden, gain_row)
    return pullback(upstream)


def adam_update(weight, moment_one, moment_two, gradient, rate, decay_rate):
    moment_one = BETA_ONE * moment_one + (1.0 - BETA_ONE) * gradient
    moment_two = BETA_TWO * moment_two + (1.0 - BETA_TWO) * gradient * gradient
    first_hat = moment_one / (1.0 - BETA_ONE**STEP)
    second_hat = moment_two / (1.0 - BETA_TWO**STEP)
    weight = weight - rate * (first_hat / (jnp.sqrt(second_hat) + ADAM_EPS) + decay_rate * weight)
    return (weight, moment_one, moment_two)


def block_count(total_rows):
    blocks = max(1, total_rows // 1024)
    while total_rows % blocks:
        blocks -= 1
    return blocks


def scores(query_blk, key_heads, live_keys):
    query_heads = query_blk.reshape(query_blk.shape[0], key_heads.shape[1], HD)
    raw_scores = jnp.einsum(
        "bhe,khe->hbk", query_heads, key_heads, preferred_element_type=FLOAT
    ) * HD ** (-0.5)
    return (jnp.where(live_keys[None, None, :], raw_scores, MASKED), query_heads)


def attention_forward(queries, key_heads, value_heads, live_keys, blocks):
    total_rows = queries.shape[0]
    block_rows = total_rows // blocks

    def one_block(query_blk):
        masked, _ = scores(query_blk, key_heads, live_keys)
        top_score = jnp.max(masked, axis=-1, keepdims=True)
        unnormed = jnp.exp(masked - top_score)
        summed = jnp.sum(unnormed, axis=-1, keepdims=True)
        weights = (unnormed / summed).astype(HALF)
        mixture = jnp.einsum("hbk,khe->bhe", weights, value_heads, preferred_element_type=FLOAT)
        return (mixture.reshape(block_rows, -1).astype(HALF), (top_score + jnp.log(summed))[..., 0])

    mixture, log_total = lax.map(one_block, queries.reshape(blocks, block_rows, -1))
    return (mixture.reshape(total_rows, -1), log_total)


def attention_backward(queries, key_heads, value_heads, live_keys, log_total, delta_mixed, blocks):
    total_rows = queries.shape[0]
    block_rows = total_rows // blocks

    def one_block(sums_kv, inputs):
        query_blk, delta_blk, total_blk = inputs
        masked, query_heads = scores(query_blk, key_heads, live_keys)
        weights = jnp.exp(masked - total_blk[..., None])
        delta_heads = delta_blk.reshape(block_rows, -1, HD)
        delta_value = sums_kv[1] + jnp.einsum(
            "hbk,bhe->khe", weights.astype(HALF), delta_heads, preferred_element_type=FLOAT
        )
        delta_weights = jnp.einsum(
            "bhe,khe->hbk", delta_heads, value_heads, preferred_element_type=FLOAT
        )
        delta_scores = weights * (
            delta_weights - jnp.sum(weights * delta_weights, axis=-1, keepdims=True)
        )
        delta_scores = delta_scores.astype(HALF) * HD ** (-0.5)
        delta_query = jnp.einsum(
            "hbk,khe->bhe", delta_scores, key_heads, preferred_element_type=FLOAT
        )
        delta_key = sums_kv[0] + jnp.einsum(
            "hbk,bhe->khe", delta_scores, query_heads, preferred_element_type=FLOAT
        )
        return ((delta_key, delta_value), delta_query.reshape(block_rows, -1).astype(HALF))

    zero_kv = jnp.zeros(key_heads.shape, FLOAT)
    (delta_key, delta_value), delta_query = lax.scan(
        one_block,
        (zero_kv, zero_kv),
        (
            queries.reshape(blocks, block_rows, -1),
            delta_mixed.reshape(blocks, block_rows, -1),
            log_total,
        ),
    )
    return (delta_query.reshape(total_rows, -1), delta_key, delta_value)


def shards(
    ctx_feat,
    qry_feat,
    counts,
    ctx_bins,
    qry_bins,
    query_mask,
    w_embed,
    w_bins,
    norm_gains,
    w_qkv,
    w_out,
    w_up,
    w_down,
    w_head,
    m_embed,
    m_bins,
    m_gains,
    m_qkv,
    m_out,
    m_up,
    m_down,
    m_head,
    v_embed,
    v_bins,
    v_gains,
    v_qkv,
    v_out,
    v_up,
    v_down,
    v_head,
):
    groups = lax.axis_size("heads")
    ctx_local = ctx_feat.shape[1]
    qry_local = qry_feat.shape[1]
    local_rows = ctx_local + qry_local
    total_rows = groups * local_rows
    model_width = w_embed.shape[1]
    local_width = w_qkv.shape[2]
    heads_here = local_width // HD
    blocks = block_count(total_rows)
    features = jnp.concatenate([ctx_feat[0], qry_feat[0]], axis=0)
    bin_hits = (ctx_bins[0][:, None] == jnp.arange(BINS)[None, :]).astype(HALF)
    bin_hits = jnp.concatenate([bin_hits, jnp.zeros((qry_local, BINS), HALF)], axis=0)
    mask_rows = query_mask[0].astype(FLOAT)
    query_count = lax.psum(jnp.sum(mask_rows), ("tables", "heads"))
    divisor = jnp.maximum(query_count, 1.0)
    embed_half = w_embed.astype(HALF)
    bins_half = w_bins.astype(HALF)
    qkv_half = w_qkv.astype(HALF)
    out_half = w_out.astype(HALF)
    up_half = w_up.astype(HALF)
    down_half = w_down.astype(HALF)
    head_half = w_head.astype(HALF)
    stream_zero = product(features, embed_half) + product(bin_hits, bins_half)
    normed_one = normalize(stream_zero, norm_gains[0]).astype(HALF)
    normed_all = lax.all_gather(normed_one, "heads", axis=0, tiled=True)
    projected = jnp.einsum(
        "rd,tdc->trc", normed_all, qkv_half, preferred_element_type=FLOAT
    ).astype(HALF)
    context = projected.reshape(3, groups, local_rows, local_width)[:, :, :ctx_local]
    context = context.reshape(3, groups * ctx_local, heads_here, HD)
    queries = projected[0]
    key_heads = context[1]
    value_heads = context[2]
    live_keys = jnp.arange(groups * ctx_local) < counts[0]
    mixture, log_total = attention_forward(queries, key_heads, value_heads, live_keys, blocks)
    attn_part = lax.psum_scatter(
        product(mixture, out_half), "heads", scatter_dimension=0, tiled=True
    )
    stream_one = stream_zero + attn_part
    normed_two = normalize(stream_one, norm_gains[1]).astype(HALF)
    second_all = lax.all_gather(normed_two, "heads", axis=0, tiled=True)
    hidden_up = product(second_all, up_half)
    active = jax.nn.gelu(hidden_up).astype(HALF)
    mlp_part = lax.psum_scatter(
        product(active, down_half), "heads", scatter_dimension=0, tiled=True
    )
    stream_two = stream_one + mlp_part
    stream_query = stream_two[ctx_local:]
    normed_final = normalize(stream_query, norm_gains[2]).astype(HALF)
    logits = product(normed_final, head_half)
    log_bins = jax.nn.logsumexp(logits, axis=-1)
    target_hits = (qry_bins[0][:, None] == jnp.arange(BINS)[None, :]).astype(FLOAT)
    loss_local = jnp.sum(mask_rows * (log_bins - jnp.sum(target_hits * logits, axis=-1)))
    back_logits = (
        mask_rows[:, None] * (jnp.exp(logits - log_bins[:, None]) - target_hits) / divisor
    ).astype(HALF)
    grad_head = jnp.einsum("rd,rb->db", normed_final, back_logits, preferred_element_type=FLOAT)
    back_final = jnp.einsum("rb,db->rd", back_logits, head_half, preferred_element_type=FLOAT)
    back_query, grad_final = norm_back(stream_query, norm_gains[2], back_final)
    back_two = jnp.concatenate([jnp.zeros((ctx_local, model_width), FLOAT), back_query], axis=0)
    back_mlp = lax.all_gather(back_two.astype(HALF), "heads", axis=0, tiled=True)
    grad_down = jnp.einsum("rf,rd->fd", active, back_mlp, preferred_element_type=FLOAT)
    back_active = jnp.einsum("rd,fd->rf", back_mlp, down_half, preferred_element_type=FLOAT)
    _, gelu_pull = jax.vjp(jax.nn.gelu, hidden_up)
    back_up = gelu_pull(back_active)[0].astype(HALF)
    grad_up = jnp.einsum("rd,rf->df", second_all, back_up, preferred_element_type=FLOAT)
    back_norm_two = lax.psum_scatter(
        jnp.einsum("rf,df->rd", back_up, up_half, preferred_element_type=FLOAT),
        "heads",
        scatter_dimension=0,
        tiled=True,
    )
    back_mid, grad_mid = norm_back(stream_one, norm_gains[1], back_norm_two)
    back_one = back_two + back_mid
    back_attn = lax.all_gather(back_one.astype(HALF), "heads", axis=0, tiled=True)
    grad_out = jnp.einsum("rc,rd->cd", mixture, back_attn, preferred_element_type=FLOAT)
    back_mix = jnp.einsum("rd,cd->rc", back_attn, out_half, preferred_element_type=FLOAT).astype(
        HALF
    )
    back_query_rows, back_key, back_value = attention_backward(
        queries, key_heads, value_heads, live_keys, log_total, back_mix, blocks
    )
    back_context = (
        jnp.stack([back_key, back_value]).astype(HALF).reshape(2, groups, ctx_local, local_width)
    )
    back_context = jnp.concatenate(
        [back_context, jnp.zeros((2, groups, qry_local, local_width), HALF)], axis=2
    )
    back_proj = jnp.concatenate(
        [back_query_rows[None], back_context.reshape(2, total_rows, local_width)], axis=0
    )
    grad_qkv = jnp.einsum("rd,trc->tdc", normed_all, back_proj, preferred_element_type=FLOAT)
    back_norm_one = lax.psum_scatter(
        jnp.einsum("trc,tdc->rd", back_proj, qkv_half, preferred_element_type=FLOAT),
        "heads",
        scatter_dimension=0,
        tiled=True,
    )
    back_first, grad_first = norm_back(stream_zero, norm_gains[0], back_norm_one)
    back_zero = (back_one + back_first).astype(HALF)
    grad_embed = jnp.einsum("rx,rd->xd", features, back_zero, preferred_element_type=FLOAT)
    grad_bins = jnp.einsum("rb,rd->bd", bin_hits, back_zero, preferred_element_type=FLOAT)
    grad_gains = jnp.stack([grad_first, grad_mid, grad_final])
    grad_qkv, grad_out, grad_up, grad_down = lax.psum(
        (grad_qkv, grad_out, grad_up, grad_down), "tables"
    )
    grad_embed, grad_bins, grad_gains, grad_head, loss_sum = lax.psum(
        (grad_embed, grad_bins, grad_gains, grad_head, loss_local), ("tables", "heads")
    )
    split_squares = (
        jnp.sum(grad_qkv * grad_qkv)
        + jnp.sum(grad_out * grad_out)
        + jnp.sum(grad_up * grad_up)
        + jnp.sum(grad_down * grad_down)
    )
    whole_squares = (
        jnp.sum(grad_embed * grad_embed)
        + jnp.sum(grad_bins * grad_bins)
        + jnp.sum(grad_gains * grad_gains)
        + jnp.sum(grad_head * grad_head)
    )
    grad_norm = jnp.sqrt(lax.psum(split_squares, "heads") + whole_squares)
    factor = jnp.minimum(1.0, CLIP_NORM / (grad_norm + 1e-06))
    embed_new, embed_first, embed_second = adam_update(
        w_embed, m_embed, v_embed, grad_embed * factor, RATE, DECAY
    )
    bins_new, bins_first, bins_second = adam_update(
        w_bins, m_bins, v_bins, grad_bins * factor, RATE_WIDE, DECAY
    )
    gains_new, gains_first, gains_second = adam_update(
        norm_gains, m_gains, v_gains, grad_gains * factor, RATE_WIDE, 0.0
    )
    qkv_new, qkv_first, qkv_second = adam_update(
        w_qkv, m_qkv, v_qkv, grad_qkv * factor, RATE, DECAY
    )
    out_new, out_first, out_second = adam_update(
        w_out, m_out, v_out, grad_out * factor, RATE_WIDE, DECAY
    )
    up_new, up_first, up_second = adam_update(w_up, m_up, v_up, grad_up * factor, RATE, DECAY)
    down_new, down_first, down_second = adam_update(
        w_down, m_down, v_down, grad_down * factor, RATE, DECAY
    )
    head_new, head_first, head_second = adam_update(
        w_head, m_head, v_head, grad_head * factor, RATE, DECAY
    )
    return (
        embed_new,
        bins_new,
        gains_new,
        qkv_new,
        out_new,
        up_new,
        down_new,
        head_new,
        embed_first,
        bins_first,
        gains_first,
        qkv_first,
        out_first,
        up_first,
        down_first,
        head_first,
        embed_second,
        bins_second,
        gains_second,
        qkv_second,
        out_second,
        up_second,
        down_second,
        head_second,
        loss_sum,
        query_count,
        grad_norm,
    )


def solution(mesh):
    in_specs = (
        P("tables", "heads", None),
        P("tables", "heads", None),
        P("tables"),
        P("tables", "heads"),
        P("tables", "heads"),
        P("tables", "heads"),
        P(),
        P(),
        P(),
        P(None, None, "heads"),
        P("heads", None),
        P(None, "heads"),
        P("heads", None),
        P(),
        P(),
        P(),
        P(),
        P(None, None, "heads"),
        P("heads", None),
        P(None, "heads"),
        P("heads", None),
        P(),
        P(),
        P(),
        P(),
        P(None, None, "heads"),
        P("heads", None),
        P(None, "heads"),
        P("heads", None),
        P(),
    )
    out_specs = (
        P(),
        P(),
        P(),
        P(None, None, "heads"),
        P("heads", None),
        P(None, "heads"),
        P("heads", None),
        P(),
        P(),
        P(),
        P(),
        P(None, None, "heads"),
        P("heads", None),
        P(None, "heads"),
        P("heads", None),
        P(),
        P(),
        P(),
        P(),
        P(None, None, "heads"),
        P("heads", None),
        P(None, "heads"),
        P("heads", None),
        P(),
        P(),
        P(),
        P(),
    )
    return jax.shard_map(shards, mesh=mesh, in_specs=in_specs, out_specs=out_specs, check_vma=False)
```

profile of v0, /device:TPU:0, one launch (start us, length us, event | category | flops | bytes accessed | tf_op | source)
XLA Modules:
  0.0 1346.1 jit_solution(15266608702587068385)
XLA Ops:
  15.9 37.4 %all-gather.5.cloned.1.call-done = bf16[2752,768]{1,0:T(8,128)(2,1)} async-done(((bf16[688,768]{1,0:T(8,128)(2,1)}), bf16[2752,768]{1,0:T(8,128)(2,1)}) %all-gather.5.cloned.1.call-update) | async-done | bytes 4227088 | tf_op jit(solution)/shard_map/all_gather | solution.py:176
  53.3 4.9 fusion.129
  59.6 6.2 reshape.248
  65.8 2.2 reshape_squeeze.4
  72.3 90.8 %while.28 = (s32[]{:T(128)}, bf16[2,1376,192]{1,2,0:T(8,128)(2,1)}, f32[2,3,1376]{2,1,0:T(4,128)S(1)}, bf16[2,1376,192]{1,2,0:T(8,128)(2,1)S(1)}, bf16[2048,3,64...) while((s32[]{:T(128)}, bf16[2,1376,192]{1,2,0:T(8,128)(2,1)}, ...), condition=%wide.region_5.6_spmd.clone, body=%wide.region_2.5_spmd.clone.sunk | while | flops 2265972736 | bytes 114830120 | solution.py:76
  73.0 13.2 fusion.186
  86.2 16.1 %fusion.187 = f32[3,1376]{1,0:T(4,128)S(1)} fusion(f32[3,1376,2048]{2,1,0:T(8,128)} %get-tuple-element.413, f32[3,1376]{1,0:T(4,128)S(1)} %get-tuple-element.414, pred[2048]{0:T(1024)(128)(4,1)S(1)} %iota_compare_fusion.7), kind=kLoop, calls=%fused_computation.6.clone.1 | loop fusion | flops 33812448 | bytes 33851648 | tf_op jit(solution)/shard_map/while/body/eval_jaxpr/reduce_sum | solution.py:71
  102.3 14.2 %fusion.188 = bf16[3,1376,64]{1,2,0:T(8,128)(2,1)S(1)} fusion(bf16[2048,3,64]{0,2,1:T(8,128)(2,1)S(1)} %get-tuple-element.448, f32[3,1376,2048]{2,1,0:T(8,128)} %get-tuple-element.413, f32[3,1376]{1,0:T(4,128)S(1)} %fusion.187, f32[3,1376]{1,0:T(4,128)S(1)} %get-tuple-element.414, pred[2048]{0:T(1024)(128)(4,1)S(1)} %iota_compare_fusion.7), kind=kOutput, calls=%fused_computation.8.clone.1 | convolution fusion | flops 1124665344 | bytes 35166464 | tf_op jit(solution)/shard_map/while/body/eval_jaxpr/hbk,khe->bhe/dot_general | solution.py:73
  118.4 13.2 fusion.186
  131.6 16.1 %fusion.187 = f32[3,1376]{1,0:T(4,128)S(1)} fusion(f32[3,1376,2048]{2,1,0:T(8,128)} %get-tuple-element.413, f32[3,1376]{1,0:T(4,128)S(1)} %get-tuple-element.414, pred[2048]{0:T(1024)(128)(4,1)S(1)} %iota_compare_fusion.7), kind=kLoop, calls=%fused_computation.6.clone.1 | loop fusion | flops 33812448 | bytes 33851648 | tf_op jit(solution)/shard_map/while/body/eval_jaxpr/reduce_sum | solution.py:71
  147.7 14.2 %fusion.188 = bf16[3,1376,64]{1,2,0:T(8,128)(2,1)S(1)} fusion(bf16[2048,3,64]{0,2,1:T(8,128)(2,1)S(1)} %get-tuple-element.448, f32[3,1376,2048]{2,1,0:T(8,128)} %get-tuple-element.413, f32[3,1376]{1,0:T(4,128)S(1)} %fusion.187, f32[3,1376]{1,0:T(4,128)S(1)} %get-tuple-element.414, pred[2048]{0:T(1024)(128)(4,1)S(1)} %iota_compare_fusion.7), kind=kOutput, calls=%fused_computation.8.clone.1 | convolution fusion | flops 1124665344 | bytes 35166464 | tf_op jit(solution)/shard_map/while/body/eval_jaxpr/hbk,khe->bhe/dot_general | solution.py:73
  163.1 3.9 copy.64
  167.0 2.8 reshape.249
  169.9 5.8 fusion.94
  175.8 72.2 %reduce-scatter.5.cloned.1.call-done = f32[688,768]{1,0:T(8,128)} async-done(((f32[2752,768]{1,0:T(8,128)}), f32[688,768]{1,0:T(8,128)}) %reduce-scatter.5.cloned.1.call-update) | async-done | bytes 2113552 | tf_op jit(solution)/shard_map/reduce_scatter | solution.py:187
  252.6 34.8 %all-gather.7.cloned.1.call-done = bf16[2752,768]{1,0:T(8,128)(2,1)} async-done(((bf16[688,768]{1,0:T(8,128)(2,1)}), bf16[2752,768]{1,0:T(8,128)(2,1)}) %all-gather.7.cloned.1.call-update) | async-done | bytes 4227088 | tf_op jit(solution)/shard_map/all_gather | solution.py:192
  287.4 6.1 fusion.83
  293.5 3.2 copy-done.80
  296.7 7.2 fusion.77
  305.2 39.8 %psum.77 = f32[]{:T(128)} all-reduce(f32[]{:T(128)} %convert_reduce_fusion), channel_id=1, replica_groups=mesh['tables'=8,'heads'=4] {'tables','heads'}, use_global_device_ids=true, to_apply=%region_15.16 | all-reduce | flops 1 | bytes 8 | tf_op jit(solution)/shard_map/psum | solution.py:165
  345.7 31.2 %reduce-scatter.7.cloned.1.call-done = f32[688,768]{1,0:T(8,128)} async-done(((f32[2752,768]{1,0:T(8,128)}), f32[688,768]{1,0:T(8,128)}) %reduce-scatter.7.cloned.1.call-update) | async-done | bytes 2113552 | tf_op jit(solution)/shard_map/reduce_scatter | solution.py:195
  383.6 34.8 %all-gather.9.cloned.1.call-done = bf16[2752,768]{1,0:T(8,128)(2,1)} async-done(((bf16[688,768]{1,0:T(8,128)(2,1)}), bf16[2752,768]{1,0:T(8,128)(2,1)}) %all-gather.9.cloned.1.call-update) | async-done | bytes 4227088 | tf_op jit(solution)/shard_map/all_gather | solution.py:212
  418.3 11.8 fusion.61
  430.2 2.0 copy-done.79
  432.1 5.7 fusion.81
  437.9 72.2 %reduce-scatter.9.cloned.1.call-done = f32[688,768]{1,0:T(8,128)} async-done(((f32[2752,768]{1,0:T(8,128)}), f32[688,768]{1,0:T(8,128)}) %reduce-scatter.9.cloned.1.call-update) | async-done | bytes 2113552 | tf_op jit(solution)/shard_map/reduce_scatter | solution.py:218
  510.2 3.0 multiply_reduce_fusion.3
  516.8 8.5 fusion.131
  525.3 10.7 fusion.111
  536.0 15.4 %all-gather.11.cloned.1.call-done = bf16[2752,768]{1,0:T(8,128)(2,1)} async-done(((bf16[688,768]{1,0:T(8,128)(2,1)}), bf16[2752,768]{1,0:T(8,128)(2,1)}) %all-gather.11.cloned.1.call-update) | async-done | bytes 4227088 | tf_op jit(solution)/shard_map/all_gather | solution.py:226
  551.4 4.7 convolution_convert_fusion
  556.1 3.0 reshape.250
  559.0 2.3 copy.66
  562.4 271.7 %while.29 = (s32[]{:T(128)}, f32[2048,3,64]{0,2,1:T(8,128)}, f32[2048,3,64]{0,2,1:T(8,128)S(1)}, bf16[2,1376,192]{1,2,0:T(8,128)(2,1)}, bf16[2,1376,192]{1,2,0:T...) while((s32[]{:T(128)}, f32[2048,3,64]{0,2,1:T(8,128)}, ...), condition=%wide.region_23.24_spmd.clone, body=%wide.region_21.23_spmd.clone.sunk | while | flops 5581586432 | bytes 255484496 | solution.py:108
  565.3 15.0 %subtract_exponential_fusion.3 = f32[3,1376,2048]{2,1,0:T(8,128)} fusion(bf16[1376,3,64]{0,2,1:T(8,128)(2,1)S(1)} %bitcast.136, bf16[2048,3,64]{0,2,1:T(8,128)(2,1)} %get-tuple-element.480, f32[3,1376]{1,0:T(4,128)S(1)} %dynamic-slice_bitcast_fusion.2, pred[2048]{0:T(1024)(128)(4,1)S(1)} %iota_compare_fusion.8), kind=kOutput, calls=%fused_computation.19.clone.1 | convolution fusion | flops 1107492864 | bytes 35149952 | tf_op jit(solution)/shard_map/while/body/eval_jaxpr/bhe,khe->hbk/dot_general | solution.py:57
  580.2 12.3 fusion.203
  592.5 16.9 %fusion.201 = f32[3,1376,2048]{2,1,0:T(8,128)} fusion(bf16[1376,3,64]{0,2,1:T(8,128)(2,1)S(1)} %bitcast.134, bf16[2048,3,64]{0,2,1:T(8,128)(2,1)} %get-tuple-element.483), kind=kOutput, calls=%fused_computation.191.clone.1 | convolution fusion | flops 1082130432 | bytes 35131392 | tf_op jit(solution)/shard_map/while/body/eval_jaxpr/bhe,khe->hbk/dot_general | solution.py:92
  609.4 43.2 %fusion.204 = bf16[3,1376,64]{1,2,0:T(8,128)(2,1)} fusion(bf16[2048,3,64]{0,2,1:T(8,128)(2,1)} %get-tuple-element.480, f32[3,1376,2048]{2,1,0:T(8,128)} %subtract_exponential_fusion.3, f32[3,1376,2048]{2,1,0:T(8,128)} %fusion.201), kind=kOutput, calls=%fused_computation.30.clone.1 | convolution fusion | flops 1150033920 | bytes 68947968 | tf_op jit(solution)/shard_map/while/body/eval_jaxpr/hbk,khe->bhe/dot_general | solution.py:99
  652.5 43.6 %fusion.202 = f32[2048,3,64]{0,2,1:T(8,128)} fusion(bf16[1376,3,64]{0,2,1:T(8,128)(2,1)S(1)} %bitcast.137, f32[3,1376,2048]{2,1,0:T(8,128)} %subtract_exponential_fusion.3, f32[3,1376,2048]{2,1,0:T(8,128)} %fusion.201, f32[2048,3,64]{0,2,1:T(8,128)} %get-tuple-element.464, pred[]{:T(512)S(6)} %compare.17), kind=kOutput, calls=%fused_computation.32.clone.1 | convolution fusion | flops 1150556160 | bytes 71307264 | tf_op jit(solution)/shard_map/while/body/eval_jaxpr/hbk,bhe->khe/dot_general | solution.py:102
  700.6 15.0 %subtract_exponential_fusion.3 = f32[3,1376,2048]{2,1,0:T(8,128)} fusion(bf16[1376,3,64]{0,2,1:T(8,128)(2,1)S(1)} %bitcast.136, bf16[2048,3,64]{0,2,1:T(8,128)(2,1)} %get-tuple-element.480, f32[3,1376]{1,0:T(4,128)S(1)} %dynamic-slice_bitcast_fusion.2, pred[2048]{0:T(1024)(128)(4,1)S(1)} %iota_compare_fusion.8), kind=kOutput, calls=%fused_computation.19.clone.1 | convolution fusion | flops 1107492864 | bytes 35149952 | tf_op jit(solution)/shard_map/while/body/eval_jaxpr/bhe,khe->hbk/dot_general | solution.py:57
  715.6 12.3 fusion.203
  727.9 16.9 %fusion.201 = f32[3,1376,2048]{2,1,0:T(8,128)} fusion(bf16[1376,3,64]{0,2,1:T(8,128)(2,1)S(1)} %bitcast.134, bf16[2048,3,64]{0,2,1:T(8,128)(2,1)} %get-tuple-element.483), kind=kOutput, calls=%fused_computation.191.clone.1 | convolution fusion | flops 1082130432 | bytes 35131392 | tf_op jit(solution)/shard_map/while/body/eval_jaxpr/bhe,khe->hbk/dot_general | solution.py:92
  744.7 43.2 %fusion.204 = bf16[3,1376,64]{1,2,0:T(8,128)(2,1)} fusion(bf16[2048,3,64]{0,2,1:T(8,128)(2,1)} %get-tuple-element.480, f32[3,1376,2048]{2,1,0:T(8,128)} %subtract_exponential_fusion.3, f32[3,1376,2048]{2,1,0:T(8,128)} %fusion.201), kind=kOutput, calls=%fused_computation.30.clone.1 | convolution fusion | flops 1150033920 | bytes 68947968 | tf_op jit(solution)/shard_map/while/body/eval_jaxpr/hbk,khe->bhe/dot_general | solution.py:99
  787.9 44.0 %fusion.202 = f32[2048,3,64]{0,2,1:T(8,128)} fusion(bf16[1376,3,64]{0,2,1:T(8,128)(2,1)S(1)} %bitcast.137, f32[3,1376,2048]{2,1,0:T(8,128)} %subtract_exponential_fusion.3, f32[3,1376,2048]{2,1,0:T(8,128)} %fusion.201, f32[2048,3,64]{0,2,1:T(8,128)} %get-tuple-element.464, pred[]{:T(512)S(6)} %compare.17), kind=kOutput, calls=%fused_computation.32.clone.1 | convolution fusion | flops 1150556160 | bytes 71307264 | tf_op jit(solution)/shard_map/while/body/eval_jaxpr/hbk,bhe->khe/dot_general | solution.py:102
  834.1 2.4 copy.67
  843.7 3.0 reshape.251
  849.5 5.6 fusion.130
  855.1 3.9 fusion.70
  860.2 8.7 convolution_bitcast_fusion
  870.7 224.4 %all-reduce.11.cloned.1.call-done = (f32[3,768,192]{1,2,0:T(8,128)}, f32[192,768]{1,0:T(8,128)}, f32[768,768]{1,0:T(8,128)}, f32[768,768]{1,0:T(8,128)}) async-done(((f32[3,768,192]{1,2,0:T(8,128)}, f32[192,768]{1,0:T(8,128)}, f32[768,768]{1,0:T(8,128)}, f32[768,768]{1,0:T(8,128)}), (f32[3,768,192]{1,2,0:T(8,128)}, f32[192,768]{1,0:T(8,128)}, f32[768,768]{1,0:T(8,128)}, ...) | async-done | bytes 7077904 | tf_op jit(solution)/shard_map/psum | solution.py:255
  1095.1 2.0 multiply_reduce_fusion.10
  1097.1 2.5 multiply_reduce_fusion.9
  1100.9 3.2 multiply_reduce_fusion.2
  1104.8 64.2 %reduce-scatter.11.cloned.1.call-done = f32[688,768]{1,0:T(8,128)} async-done(((f32[2752,768]{1,0:T(8,128)}), f32[688,768]{1,0:T(8,128)}) %reduce-scatter.11.cloned.1.call-update) | async-done | bytes 2113552 | tf_op jit(solution)/shard_map/reduce_scatter | solution.py:244
  1169.1 2.4 multiply_reduce_fusion.4
  1178.2 6.3 psum.83
  1184.4 40.7 %all-reduce.3 = (f32[3,768]{1,0:T(4,128)S(1)}, f32[]{:T(128)}) all-reduce(f32[3,768]{1,0:T(4,128)S(1)} %pad_maximum_fusion.3, f32[]{:T(128)} %get-tuple-element.289), channel_id=1, replica_groups=mesh['tables'=8,'heads'=4] {'tables','heads'}, use_global_device_ids=true, to_apply=%region_43.44 | all-reduce | flops 2305 | bytes 18440 | tf_op jit(solution)/shard_map/psum | solution.py:258
  1225.8 80.1 %all-reduce.9.cloned.1.call-done = (f32[100,768]{1,0:T(8,128)}, f32[64,768]{1,0:T(8,128)}, f32[768,64]{0,1:T(8,128)}) async-done(((f32[100,768]{1,0:T(8,128)}, f32[64,768]{1,0:T(8,128)}, f32[768,64]{0,1:T(8,128)}), (f32[100,768]{1,0:T(8,128)}, f32[64,768]{1,0:T(8,128)}, f32[768,64]{0,1:T(8,128)})) %all-reduce.9.cloned.1.call-update) | async-done | bytes 700432 | tf_op jit(solution)/shard_map/psum | solution.py:258
  1314.7 2.2 multiply_subtract_fusion.4
  1316.8 2.1 add_subtract_fusion.1
  1319.0 2.3 multiply_subtract_fusion.3
  1321.3 2.9 add_subtract_fusion
  1324.2 5.6 multiply_subtract_fusion.2
  1331.6 6.3 multiply_subtract_fusion
  (281 shorter events, 70.4 us)
Async XLA Ops:
  7.2 4.8 copy-start.48
  7.2 46.1 %all-gather.5.cloned.1.call-start = ((), (), s32[]{:S(2)}) async-start(), calls=%async_computation.4 | async-start | bytes 5283840 | tf_op jit(solution)/shard_map/all_gather | solution.py:176
  8.7 5.1 copy-start.60
  9.6 2.9 copy-start.51
  15.7 232.2 %reduce-scatter.5.cloned.1.call-start = ((), (), s32[]{:S(2)}) async-start(), calls=%async_computation.5 | async-start | bytes 10567680 | tf_op jit(solution)/shard_map/reduce_scatter | solution.py:187
  15.9 42.3 %copy-start.46 = (bf16[3,768,192]{1,2,0:T(8,128)(2,1)}, bf16[3,768,192]{1,2,0:T(8,128)(2,1)S(1)}, u32[]{:S(2)}) copy-start(bf16[3,768,192]{1,2,0:T(8,128)(2,1)S(1)} %convert_element_type.119) | copy-start | bytes 2654212
  102.3 14.3 %copy-start.24 = (bf16[2,1376,192]{1,2,0:T(8,128)(2,1)S(1)}, bf16[2,1376,192]{1,2,0:T(8,128)(2,1)}, u32[]{:S(2)}) copy-start(bf16[2,1376,192]{1,2,0:T(8,128)(2,1)} %get-tuple-element.436) | copy-start | bytes 3170308 | tf_op jit(solution)/shard_map/while
  147.7 14.3 %copy-start.24 = (bf16[2,1376,192]{1,2,0:T(8,128)(2,1)S(1)}, bf16[2,1376,192]{1,2,0:T(8,128)(2,1)}, u32[]{:S(2)}) copy-start(bf16[2,1376,192]{1,2,0:T(8,128)(2,1)} %get-tuple-element.436) | copy-start | bytes 3170308 | tf_op jit(solution)/shard_map/while
  163.1 12.6 copy-start.5
  163.1 12.6 copy-start.6
  163.1 6.8 copy-start.37
  175.7 72.3 %copy-start.1 = (f32[688,768]{1,0:T(8,128)S(1)}, f32[688,768]{1,0:T(8,128)}, u32[]{:S(2)}) copy-start(f32[688,768]{1,0:T(8,128)} %copy-done) | copy-start | bytes 6340612
  175.7 75.5 %copy-start.62 = (f32[768]{0:T(1024)S(1)}, f32[768]{0:T(1024)}, u32[]{:S(2)}) copy-start(f32[768]{0:T(1024)} %get-tuple-element.220) | copy-start | bytes 9220
  175.7 111.6 %all-gather.7.cloned.1.call-start = ((), (), s32[]{:S(2)}) async-start(), calls=%async_computation.6 | async-start | bytes 5283840 | tf_op jit(solution)/shard_map/all_gather | solution.py:192
  252.5 44.2 %copy-start.28 = (f32[768,768]{1,0:T(8,128)S(1)}, f32[768,768]{1,0:T(8,128)}, u32[]{:S(2)}) copy-start(f32[768,768]{1,0:T(8,128)} %param.46) | copy-start | bytes 7077892
  252.5 124.4 %reduce-scatter.7.cloned.1.call-start = ((), (), s32[]{:S(2)}) async-start(), calls=%async_computation.7 | async-start | bytes 10567680 | tf_op jit(solution)/shard_map/reduce_scatter | solution.py:195
  293.4 3.2 copy-start.80
  303.9 73.0 %copy-start.4 = (f32[688,768]{1,0:T(8,128)S(1)}, f32[688,768]{1,0:T(8,128)}, u32[]{:S(2)}) copy-start(f32[688,768]{1,0:T(8,128)} %copy-done.3) | copy-start | bytes 6340612
  303.9 74.4 %copy-start.57 = (f32[768]{0:T(1024)S(1)}, f32[768]{0:T(1024)}, u32[]{:S(2)}) copy-start(f32[768]{0:T(1024)} %get-tuple-element.219) | copy-start | bytes 9220
  304.0 75.3 %copy-start.40 = (f32[768,64]{0,1:T(8,128)S(1)}, f32[768,64]{0,1:T(8,128)}, u32[]{:S(2)}) copy-start(f32[768,64]{0,1:T(8,128)} %param.47) | copy-start | bytes 589828
  304.0 75.5 %copy-start.74 = (s32[1,176]{1,0:T(1,128)S(1)}, s32[1,176]{1,0:T(1,128)}, u32[]{:S(2)}) copy-start(s32[1,176]{1,0:T(1,128)} %param.38) | copy-start | bytes 2116
  304.0 114.3 %all-gather.9.cloned.1.call-start = ((), (), s32[]{:S(2)}) async-start(), calls=%async_computation.8 | async-start | bytes 5283840 | tf_op jit(solution)/shard_map/all_gather | solution.py:212
  345.1 36.1 %copy-start.70 = (f32[1,176]{1,0:T(1,128)}, f32[1,176]{1,0:T(1,128)S(1)}, u32[]{:S(2)}) copy-start(f32[1,176]{1,0:T(1,128)S(1)} %convert_element_type.114) | copy-start | bytes 2116
  380.2 3.3 copy-start.76
  383.5 126.7 %reduce-scatter.9.cloned.1.call-start = ((), (), s32[]{:S(2)}) async-start(), calls=%async_computation.9 | async-start | bytes 10567680 | tf_op jit(solution)/shard_map/reduce_scatter | solution.py:218
  418.3 13.8 %copy-start.30 = (f32[768,768]{1,0:T(8,128)S(1)}, f32[768,768]{1,0:T(8,128)}, u32[]{:S(2)}) copy-start(f32[768,768]{1,0:T(8,128)} %param.45) | copy-start | bytes 7077892
  437.9 113.5 %all-gather.11.cloned.1.call-start = ((), (), s32[]{:S(2)}) async-start(), calls=%async_computation.10 | async-start | bytes 5283840 | tf_op jit(solution)/shard_map/all_gather | solution.py:226
  510.2 3.0 copy-start.19
  513.2 2.2 copy-start.16
  514.1 2.5 copy-start.66
  516.6 578.5 %all-reduce.11.cloned.1.call-start = ((), (), s32[]{:S(2)}) async-start(), calls=%async_computation.13 | async-start | bytes 14155776 | tf_op jit(solution)/shard_map/psum | solution.py:255
  525.3 26.1 %copy-start.38 = (f32[192,768]{1,0:T(8,128)S(1)}, f32[192,768]{1,0:T(8,128)}, u32[]{:S(2)}) copy-start(f32[192,768]{1,0:T(8,128)} %param.44) | copy-start | bytes 1769476
  609.4 43.2 %copy-start.10 = (bf16[1,1376,192]{1,2,0:T(8,128)(2,1)S(1)}, bf16[1,1376,192]{1,2,0:T(8,128)(2,1)}, u32[]{:S(2)}) copy-start(bf16[1,1376,192]{1,2,0:T(8,128)(2,1)} %copy-done.9) | copy-start | bytes 1585156 | tf_op jit(solution)/shard_map/while
  744.7 43.2 %copy-start.10 = (bf16[1,1376,192]{1,2,0:T(8,128)(2,1)S(1)}, bf16[1,1376,192]{1,2,0:T(8,128)(2,1)}, u32[]{:S(2)}) copy-start(bf16[1,1376,192]{1,2,0:T(8,128)(2,1)} %copy-done.9) | copy-start | bytes 1585156 | tf_op jit(solution)/shard_map/while
  843.7 3.0 copy-start.23
  843.7 11.4 slice-start
  848.3 6.8 slice-start.1
  849.5 5.6 copy-start.54
  859.0 310.0 %reduce-scatter.11.cloned.1.call-start = ((), (), s32[]{:S(2)}) async-start(), calls=%async_computation.11 | async-start | bytes 10567680 | tf_op jit(solution)/shard_map/reduce_scatter | solution.py:244
  868.9 437.0 %all-reduce.9.cloned.1.call-start = ((), (), s32[]{:S(2)}) async-start(), calls=%async_computation.12 | async-start | bytes 1425408 | tf_op jit(solution)/shard_map/psum | solution.py:258
  1095.1 74.0 %copy-start.2 = (f32[688,768]{1,0:T(8,128)S(1)}, f32[688,768]{1,0:T(8,128)}, u32[]{:S(2)}) copy-start(f32[688,768]{1,0:T(8,128)} %copy-done) | copy-start | bytes 6340612
  1095.1 74.0 %copy-start.56 = (f32[688]{0:T(1024)S(1)}, f32[688]{0:T(1024)}, u32[]{:S(2)}) copy-start(f32[688]{0:T(1024)} %copy-done.55) | copy-start | bytes 8260
  1095.1 74.0 %copy-start.59 = (f32[688]{0:T(1024)S(1)}, f32[688]{0:T(1024)}, u32[]{:S(2)}) copy-start(f32[688]{0:T(1024)} %copy-done.58) | copy-start | bytes 8260
  1095.1 74.0 %copy-start.61 = (f32[768]{0:T(1024)S(1)}, f32[768]{0:T(1024)}, u32[]{:S(2)}) copy-start(f32[768]{0:T(1024)} %copy-done.60) | copy-start | bytes 9220
  1104.1 67.4 %copy-start.65 = (f32[688]{0:T(1024)S(1)}, f32[688]{0:T(1024)}, u32[]{:S(2)}) copy-start(f32[688]{0:T(1024)} %copy-done.64) | copy-start | bytes 8260
  1169.0 2.5 copy-start.18
  1175.1 3.0 copy-start.68
  1175.1 138.9 %copy-start.63 = (f32[3,768]{1,0:T(4,128)S(1)}, f32[3,768]{1,0:T(4,128)}, u32[]{:S(2)}) copy-start(f32[3,768]{1,0:T(4,128)} %param.42) | copy-start | bytes 27652
  1175.1 138.9 %copy-start.72 = (f32[3,768]{1,0:T(4,128)S(1)}, f32[3,768]{1,0:T(4,128)}, u32[]{:S(2)}) copy-start(f32[3,768]{1,0:T(4,128)} %param.50) | copy-start | bytes 27652
  1175.1 138.9 %copy-start.73 = (f32[3,768]{1,0:T(4,128)S(1)}, f32[3,768]{1,0:T(4,128)}, u32[]{:S(2)}) copy-start(f32[3,768]{1,0:T(4,128)} %param.58) | copy-start | bytes 27652
  1176.2 138.5 %copy-start.41 = (f32[768,64]{0,1:T(8,128)S(1)}, f32[768,64]{0,1:T(8,128)}, u32[]{:S(2)}) copy-start(f32[768,64]{0,1:T(8,128)} %param.47) | copy-start | bytes 589828
  1176.2 145.1 %copy-start.39 = (f32[192,768]{1,0:T(8,128)S(1)}, f32[192,768]{1,0:T(8,128)}, u32[]{:S(2)}) copy-start(f32[192,768]{1,0:T(8,128)} %param.44) | copy-start | bytes 1769476
  1177.4 141.5 %copy-start.42 = (f32[100,768]{1,0:T(8,128)S(1)}, f32[100,768]{1,0:T(8,128)}, u32[]{:S(2)}) copy-start(f32[100,768]{1,0:T(8,128)} %param.40) | copy-start | bytes 921604
  1314.0 4.9 copy-start.43
  1314.7 6.6 copy-start.36
  1314.7 15.1 %copy-start.35 = (f32[768,768]{1,0:T(8,128)S(1)}, f32[768,768]{1,0:T(8,128)}, u32[]{:S(2)}) copy-start(f32[768,768]{1,0:T(8,128)} %param.53) | copy-start | bytes 7077892
  1319.0 10.8 copy-start.34
  1321.3 2.9 copy-start.21
  1321.3 2.9 copy-start.22
  1324.2 5.6 copy-start.12
  1324.2 5.6 copy-start.29
  1324.2 5.6 copy-start.31
  1324.2 6.7 copy-start.32
  1324.2 7.4 copy-start.33
  (33 other events, 41.5 us)
Sparse Core Ops, SparseCore 0:
  15.9 37.3 all-gather.4
  175.8 72.0 reduce-scatter.4
  252.6 34.6 all-gather.6
  304.1 72.8 reduce-scatter.6
  383.6 34.6 all-gather.8
  438.0 72.1 reduce-scatter.8
  516.7 34.6 all-gather.10
  859.1 235.8 all-reduce.10
  1097.9 71.1 reduce-scatter.10
  1176.6 129.2 all-reduce.8
where the time goes:
time: 1350 us
  waiting for transfers between devices  667 us (49%)
  matrix products  407 us (30%)
  other arithmetic  93.2 us (7%)
  blocking collectives  86.8 us (6%)
  local copies, waits for them, and re-layouts  67.9 us (5%)
  between operations  23.1 us (2%)
    psum x1, waiting for transfers between devices, shards(): lax.psum((grad_qkv, grad_out, grad_up, grad_down), 'tables')  224 us
    dot_general x2, matrix products, one_block(): jnp.einsum('hbk,bhe->khe', delta_scores, query_heads, preferred_element_t...  87.5 us
    dot_general x2, matrix products, one_block(): jnp.einsum('hbk,khe->bhe', delta_scores, key_heads, preferred_element_typ...  86.3 us
    psum x1, waiting for transfers between devices, shards(): lax.psum((grad_embed, grad_bins, grad_gains, grad_head, loss_local), ('ta...  80.1 us
    reduce_scatter x1, waiting for transfers between devices, shards(): lax.psum_scatter(jnp.einsum('rf,df->rd', back_up, up_half, preferred_elem...  72.2 us
    reduce_scatter x1, waiting for transfers between devices, shards(): lax.psum_scatter(product(mixture, out_half), 'heads', scatter_dimension=0...  72.2 us
    reduce_scatter x1, waiting for transfers between devices, shards(): lax.psum_scatter(jnp.einsum('trc,tdc->rd', back_proj, qkv_half, preferred...  64.2 us
    dot_general x4, matrix products, scores(): jnp.einsum('bhe,khe->hbk', query_heads, key_heads, preferred_element_type...  56.4 us
  transfers between devices with their start and end apart: 10, of which 10 were waited for; matrix products, arithmetic and copies ran while one was open for 3% of the time, Pallas kernels for 0%

commit v1 on v0

v1 whole, which is shorter than its diff:
```python
import jax
import jax.numpy as jnp
from jax import lax
from jax.sharding import PartitionSpec as P

HD = 64
BINS = 64
STEP = 10


NORM_EPS = 1e-05
ADAM_EPS = 1e-08
RATE = 0.05
RATE_WIDE = 1.0
BETA_ONE = 0.9
BETA_TWO = 0.95
DECAY = 0.1
CLIP_NORM = 0.02
MASKED = -1e30
FLOAT = jnp.float32
HALF = jnp.bfloat16


def product(left, right):
    return jnp.dot(left, right, preferred_element_type=FLOAT)


def normalize(hidden, gain_row):
    center = hidden - jnp.mean(hidden, axis=-1, keepdims=True)
    spread = jnp.mean(center * center, axis=-1, keepdims=True)
    return center * lax.rsqrt(spread + NORM_EPS) * gain_row


def norm_back(hidden, gain_row, upstream):
    _, pullback = jax.vjp(normalize, hidden, gain_row)
    return pullback(upstream)


def adam_update(weight, moment_one, moment_two, gradient, rate, decay_rate):
    moment_one = BETA_ONE * moment_one + (1.0 - BETA_ONE) * gradient
    moment_two = BETA_TWO * moment_two + (1.0 - BETA_TWO) * gradient * gradient
    first_hat = moment_one / (1.0 - BETA_ONE**STEP)
    second_hat = moment_two / (1.0 - BETA_TWO**STEP)
    weight = weight - rate * (first_hat / (jnp.sqrt(second_hat) + ADAM_EPS) + decay_rate * weight)
    return (weight, moment_one, moment_two)


def softmax_rows(query_heads, key_heads, live_keys):
    raw_scores = jnp.einsum(
        "bhe,khe->hbk", query_heads, key_heads, preferred_element_type=FLOAT
    ) * HD ** (-0.5)
    masked = jnp.where(live_keys[None, None, :], raw_scores, MASKED)
    top_score = jnp.max(masked, axis=-1, keepdims=True)
    unnormed = jnp.exp(masked - top_score)
    return unnormed / jnp.sum(unnormed, axis=-1, keepdims=True)


def gather(rows, axis=0):
    return lax.all_gather(rows, "heads", axis=axis, tiled=True)


def shards(
    ctx_feat,
    qry_feat,
    counts,
    ctx_bins,
    qry_bins,
    query_mask,
    w_embed,
    w_bins,
    norm_gains,
    w_qkv,
    w_out,
    w_up,
    w_down,
    w_head,
    m_embed,
    m_bins,
    m_gains,
    m_qkv,
    m_out,
    m_up,
    m_down,
    m_head,
    v_embed,
    v_bins,
    v_gains,
    v_qkv,
    v_out,
    v_up,
    v_down,
    v_head,
):
    model_width = w_embed.shape[1]
    heads_here = w_qkv.shape[2] // HD
    me = lax.axis_index("heads")
    qry_local = qry_feat.shape[1]
    ctx_rows = gather(ctx_feat[0])
    qry_rows = gather(qry_feat[0])
    all_bins = gather(jnp.concatenate([ctx_bins[0], qry_bins[0], query_mask[0]]).reshape(1, -1))
    ctx_local = ctx_feat.shape[1]
    all_ctx_bins = all_bins[:, :ctx_local].reshape(-1)
    all_qry_bins = all_bins[:, ctx_local : ctx_local + qry_local].reshape(-1)
    mask_rows = all_bins[:, ctx_local + qry_local :].reshape(-1).astype(FLOAT)
    total_ctx = ctx_rows.shape[0]
    total_qry = qry_rows.shape[0]
    bin_hits = (all_ctx_bins[:, None] == jnp.arange(BINS)[None, :]).astype(HALF)
    query_count = lax.psum(jnp.sum(mask_rows), "tables")
    divisor = jnp.maximum(query_count, 1.0)
    embed_half = w_embed.astype(HALF)
    bins_half = w_bins.astype(HALF)
    qkv_half = w_qkv.astype(HALF)
    out_half = w_out.astype(HALF)
    up_half = w_up.astype(HALF)
    down_half = w_down.astype(HALF)
    head_half = w_head.astype(HALF)
    out_full = gather(out_half)
    zero_ctx = product(ctx_rows, embed_half) + product(bin_hits, bins_half)
    zero_qry = product(qry_rows, embed_half)
    normed_ctx = normalize(zero_ctx, norm_gains[0]).astype(HALF)
    normed_qry = normalize(zero_qry, norm_gains[0]).astype(HALF)
    queries = product(normed_qry, qkv_half[0]).astype(HALF).reshape(total_qry, heads_here, HD)
    key_heads = product(normed_ctx, qkv_half[1]).astype(HALF).reshape(total_ctx, heads_here, HD)
    value_heads = product(normed_ctx, qkv_half[2]).astype(HALF).reshape(total_ctx, heads_here, HD)
    live_keys = jnp.arange(total_ctx) < counts[0]
    weights = softmax_rows(queries, key_heads, live_keys)
    mixture = jnp.einsum(
        "hbk,khe->bhe", weights.astype(HALF), value_heads, preferred_element_type=FLOAT
    )
    mixture = mixture.reshape(total_qry, -1).astype(HALF)
    stream_one = zero_qry + product(gather(mixture, 1), out_full)
    normed_two = normalize(stream_one, norm_gains[1]).astype(HALF)
    hidden_up = product(normed_two, up_half)
    active = jax.nn.gelu(hidden_up).astype(HALF)
    mlp = lax.psum(product(active, down_half).astype(HALF), "heads")
    stream_two = stream_one + mlp.astype(FLOAT)
    normed_final = normalize(stream_two, norm_gains[2]).astype(HALF)
    logits = product(normed_final, head_half)
    log_bins = jax.nn.logsumexp(logits, axis=-1)
    target_hits = (all_qry_bins[:, None] == jnp.arange(BINS)[None, :]).astype(FLOAT)
    loss_local = jnp.sum(mask_rows * (log_bins - jnp.sum(target_hits * logits, axis=-1)))
    back_logits = (
        mask_rows[:, None] * (jnp.exp(logits - log_bins[:, None]) - target_hits) / divisor
    ).astype(HALF)
    grad_head = jnp.einsum("rd,rb->db", normed_final, back_logits, preferred_element_type=FLOAT)
    back_final = jnp.einsum("rb,db->rd", back_logits, head_half, preferred_element_type=FLOAT)
    back_two, grad_final = norm_back(stream_two, norm_gains[2], back_final)
    back_mlp = back_two.astype(HALF)
    grad_down = jnp.einsum("rf,rd->fd", active, back_mlp, preferred_element_type=FLOAT)
    back_active = jnp.einsum("rd,fd->rf", back_mlp, down_half, preferred_element_type=FLOAT)
    _, gelu_pull = jax.vjp(jax.nn.gelu, hidden_up)
    back_up = gelu_pull(back_active)[0].astype(HALF)
    grad_up = jnp.einsum("rd,rf->df", normed_two, back_up, preferred_element_type=FLOAT)
    back_norm_two = jnp.einsum("rf,df->rd", back_up, up_half, preferred_element_type=FLOAT)
    back_norm_two = lax.psum(back_norm_two.astype(HALF), "heads").astype(FLOAT)
    back_mid, grad_mid = norm_back(stream_one, norm_gains[1], back_norm_two)
    back_one = back_two + back_mid
    back_attn = back_one.astype(HALF)
    grad_out = jnp.einsum("rc,rd->cd", mixture, back_attn, preferred_element_type=FLOAT)
    back_mix = jnp.einsum("rd,cd->rc", back_attn, out_half, preferred_element_type=FLOAT)
    back_mix = back_mix.astype(HALF).reshape(total_qry, heads_here, HD)
    back_value = jnp.einsum(
        "hbk,bhe->khe", weights.astype(HALF), back_mix, preferred_element_type=FLOAT
    )
    back_weights = jnp.einsum("bhe,khe->hbk", back_mix, value_heads, preferred_element_type=FLOAT)
    back_scores = weights * (
        back_weights - jnp.sum(weights * back_weights, axis=-1, keepdims=True)
    )
    back_scores = back_scores.astype(HALF) * HD ** (-0.5)
    back_query = jnp.einsum("hbk,khe->bhe", back_scores, key_heads, preferred_element_type=FLOAT)
    back_key = jnp.einsum("hbk,bhe->khe", back_scores, queries, preferred_element_type=FLOAT)
    back_query = back_query.reshape(total_qry, -1).astype(HALF)
    back_key = back_key.reshape(total_ctx, -1).astype(HALF)
    back_value = back_value.reshape(total_ctx, -1).astype(HALF)
    grad_qkv = jnp.stack(
        [
            jnp.einsum("rd,rc->dc", normed_qry, back_query, preferred_element_type=FLOAT),
            jnp.einsum("rd,rc->dc", normed_ctx, back_key, preferred_element_type=FLOAT),
            jnp.einsum("rd,rc->dc", normed_ctx, back_value, preferred_element_type=FLOAT),
        ]
    )
    part_qry = jnp.einsum("rc,dc->rd", back_query, qkv_half[0], preferred_element_type=FLOAT)
    part_ctx = jnp.einsum(
        "rc,dc->rd", back_key, qkv_half[1], preferred_element_type=FLOAT
    ) + jnp.einsum("rc,dc->rd", back_value, qkv_half[2], preferred_element_type=FLOAT)
    first_qry, gain_qry = norm_back(zero_qry, norm_gains[0], part_qry)
    first_ctx, gain_ctx = norm_back(zero_ctx, norm_gains[0], part_ctx)
    mine = (jnp.arange(total_qry) // qry_local == me)[:, None]
    back_qry = (first_qry + jnp.where(mine, back_one, 0.0)).astype(HALF)
    back_ctx = first_ctx.astype(HALF)
    grad_embed = jnp.einsum(
        "rx,rd->xd", qry_rows, back_qry, preferred_element_type=FLOAT
    ) + jnp.einsum("rx,rd->xd", ctx_rows, back_ctx, preferred_element_type=FLOAT)
    grad_bins = jnp.einsum("rb,rd->bd", bin_hits, back_ctx, preferred_element_type=FLOAT)
    grad_qkv, grad_out, grad_up, grad_down = [
        total.astype(FLOAT)
        for total in lax.psum(
            tuple(part.astype(HALF) for part in (grad_qkv, grad_out, grad_up, grad_down)), "tables"
        )
    ]
    grad_embed, grad_bins, grad_first = lax.psum(
        (grad_embed, grad_bins, gain_qry + gain_ctx), ("tables", "heads")
    )
    grad_head, grad_mid, grad_final, loss_sum = lax.psum(
        (grad_head, grad_mid, grad_final, loss_local), "tables"
    )
    grad_gains = jnp.stack([grad_first, grad_mid, grad_final])
    split_squares = (
        jnp.sum(grad_qkv * grad_qkv)
        + jnp.sum(grad_out * grad_out)
        + jnp.sum(grad_up * grad_up)
        + jnp.sum(grad_down * grad_down)
    )
    whole_squares = (
        jnp.sum(grad_embed * grad_embed)
        + jnp.sum(grad_bins * grad_bins)
        + jnp.sum(grad_gains * grad_gains)
        + jnp.sum(grad_head * grad_head)
    )
    grad_norm = jnp.sqrt(lax.psum(split_squares, "heads") + whole_squares)
    factor = jnp.minimum(1.0, CLIP_NORM / (grad_norm + 1e-06))
    embed_new, embed_first, embed_second = adam_update(
        w_embed, m_embed, v_embed, grad_embed * factor, RATE, DECAY
    )
    bins_new, bins_first, bins_second = adam_update(
        w_bins, m_bins, v_bins, grad_bins * factor, RATE_WIDE, DECAY
    )
    gains_new, gains_first, gains_second = adam_update(
        norm_gains, m_gains, v_gains, grad_gains * factor, RATE_WIDE, 0.0
    )
    qkv_new, qkv_first, qkv_second = adam_update(
        w_qkv, m_qkv, v_qkv, grad_qkv * factor, RATE, DECAY
    )
    out_new, out_first, out_second = adam_update(
        w_out, m_out, v_out, grad_out * factor, RATE_WIDE, DECAY
    )
    up_new, up_first, up_second = adam_update(w_up, m_up, v_up, grad_up * factor, RATE, DECAY)
    down_new, down_first, down_second = adam_update(
        w_down, m_down, v_down, grad_down * factor, RATE, DECAY
    )
    head_new, head_first, head_second = adam_update(
        w_head, m_head, v_head, grad_head * factor, RATE, DECAY
    )
    return (
        embed_new,
        bins_new,
        gains_new,
        qkv_new,
        out_new,
        up_new,
        down_new,
        head_new,
        embed_first,
        bins_first,
        gains_first,
        qkv_first,
        out_first,
        up_first,
        down_first,
        head_first,
        embed_second,
        bins_second,
        gains_second,
        qkv_second,
        out_second,
        up_second,
        down_second,
        head_second,
        loss_sum,
        query_count,
        grad_norm,
    )


def solution(mesh):
    in_specs = (
        P("tables", "heads", None),
        P("tables", "heads", None),
        P("tables"),
        P("tables", "heads"),
        P("tables", "heads"),
        P("tables", "heads"),
        P(),
        P(),
        P(),
        P(None, None, "heads"),
        P("heads", None),
        P(None, "heads"),
        P("heads", None),
        P(),
        P(),
        P(),
        P(),
        P(None, None, "heads"),
        P("heads", None),
        P(None, "heads"),
        P("heads", None),
        P(),
        P(),
        P(),
        P(),
        P(None, None, "heads"),
        P("heads", None),
        P(None, "heads"),
        P("heads", None),
        P(),
    )
    out_specs = (
        P(),
        P(),
        P(),
        P(None, None, "heads"),
        P("heads", None),
        P(None, "heads"),
        P("heads", None),
        P(),
        P(),
        P(),
        P(),
        P(None, None, "heads"),
        P("heads", None),
        P(None, "heads"),
        P("heads", None),
        P(),
        P(),
        P(),
        P(),
        P(None, None, "heads"),
        P("heads", None),
        P(None, "heads"),
        P("heads", None),
        P(),
        P(),
        P(),
        P(),
    )
    return jax.shard_map(shards, mesh=mesh, in_specs=in_specs, out_specs=out_specs, check_vma=False)
```

time: 1350 us -> 667 us (0.49)
  waiting for transfers between devices: 667 us -> 293 us
  matrix products: 407 us -> 142 us
  local copies, waits for them, and re-layouts: 67.9 us -> 17.8 us
  other arithmetic: 93.2 us -> 54.2 us
  blocking collectives: 86.8 us -> 116 us
    reduce_scatter x4 -> x0, waiting for transfers between devices: 240 us -> none  [the longest x1 72.2 us: shards(): lax.psum_scatter(jnp.einsum('rf,df->rd', back_up, up_half, preferred_elem...]
    dot_general x19 -> x15, matrix products: 340 us -> 105 us  [the longest x1 29.1 us: shards(): jnp.einsum('hbk,khe->bhe', back_scores, key_heads, preferred_element_type...]
    all_gather x4 -> x2, waiting for transfers between devices: 122 us -> 36.8 us  [gather(): return lax.all_gather(rows, 'heads', axis=axis, tiled=True)]
    psum x2 -> x5, waiting for transfers between devices: 304 us -> 256 us  [the longest x1 140 us: shards(): lax.psum(tuple((part.astype(HALF) for part in (grad_qkv, grad_out, grad_u...]
    reduce_sum x4 -> x0, other arithmetic: 34 us -> none  [the longest x2 32.2 us: one_block(): summed = jnp.sum(unnormed, axis=-1, keepdims=True)]
    reshape x7 -> x0, local copies, waits for them, and re-layouts: 15 us -> none  [the longest x1 6.21 us: shards(): projected.reshape(3, groups, local_rows, local_width)[:, :, :ctx_local]]
    psum x2 -> x3, blocking collectives: 80.6 us -> 83.8 us  [the longest x1 39.8 us: shards(): lax.psum((grad_embed, grad_bins, gain_qry + gain_ctx), ('tables', 'heads'))]
  transfers between devices with their start and end apart: 10 -> 7, of which waited for: 10 -> 6; matrix products, arithmetic and copies ran while one was open for 3% -> 18% of each run, Pallas kernels for 0% -> 0%
where the time goes in v1:
time: 667 us; the launch traced here: 657 us
  waiting for transfers between devices  293 us (44%)
  matrix products  142 us (21%)
  blocking collectives  116 us (17%)
  other arithmetic  54.2 us (8%)
  between operations  24.6 us (4%)
  local copies, waits for them, and re-layouts  17.8 us (3%)
  starting transfers between devices  9.84 us (1%)
    psum x1, waiting for transfers between devices, shards(): lax.psum(tuple((part.astype(HALF) for part in (grad_qkv, grad_out, grad_u...  140 us
    psum x1, waiting for transfers between devices, shards(): lax.psum((grad_embed, grad_bins, gain_qry + gain_ctx), ('tables', 'heads'))  63.3 us
    psum x1, blocking collectives, shards(): lax.psum((grad_embed, grad_bins, gain_qry + gain_ctx), ('tables', 'heads'))  39.8 us
    all_gather x2, waiting for transfers between devices, gather(): return lax.all_gather(rows, 'heads', axis=axis, tiled=True)  36.8 us
    psum x1, waiting for transfers between devices, shards(): mlp = lax.psum(product(active, down_half).astype(HALF), 'heads')  35.7 us
    dot_general x1, matrix products, shards(): jnp.einsum('hbk,khe->bhe', back_scores, key_heads, preferred_element_type...  29.1 us
    dot_general x1, matrix products, shards(): jnp.einsum('hbk,bhe->khe', back_scores, queries, preferred_element_type=F...  26.8 us
    psum x1, blocking collectives, shards(): lax.psum((grad_head, grad_mid, grad_final, loss_local), 'tables')  22 us
  transfers between devices with their start and end apart: 7, of which 6 were waited for; matrix products, arithmetic and copies ran while one was open for 18% of the time, Pallas kernels for 0%

profile of v1, /device:TPU:0, one launch (start us, length us, event | category | flops | bytes accessed | tf_op | source)
XLA Modules:
  0.0 657.3 jit_solution(13079810308067233948)
XLA Ops:
  8.1 1.2 dynamic-slice
  10.9 12.7 %all-reduce = s32[3456]{0:T(1024)S(1)} all-reduce(s32[3456]{0:T(1024)S(1)} %add_dynamic-update-slice_fusion), channel_id=3, replica_groups=mesh['tables'=8,'heads'=4] {'heads'}, use_global_device_ids=true, to_apply=%add | all-reduce | flops 3456 | bytes 27648
  23.7 6.5 all-gather
  30.2 1.7 convert_element_type.168
  33.1 1.1 fusion.154
  34.9 1.9 copy-done
  40.0 5.6 all-gather.2
  48.5 8.8 %fusion.155 = (f32[3,704]{1,0:T(4,128)S(1)}, f32[3,704,2048]{2,1,0:T(8,128)}) fusion(pred[2048]{0:T(1024)(128)(4,1)S(1)} %iota_compare_fusion.3, bf16[704,3,64]{0,2,1:T(8,128)(2,1)S(1)} %bitcast.112, bf16[2048,3,64]{0,2,1:T(8,128)(2,1)S(1)} %bitcast.105), kind=kOutput, calls=%fused_computation.238 | convolution fusion | flops 570951680 | bytes 18368768 | tf_op jit(solution)/shard_map/sub | solution.py:54
  57.3 9.4 %fusion.60 = bf16[3,64,704]{2,1,0:T(8,128)(2,1)} fusion(bf16[2048,3,64]{0,2,1:T(8,128)(2,1)S(1)} %bitcast.93, f32[3,704,2048]{2,1,0:T(8,128)} %get-tuple-element.92, f32[3,704]{1,0:T(4,128)S(1)} %get-tuple-element.91), kind=kOutput, calls=%fused_computation.97 | convolution fusion | flops 562434048 | bytes 18366720 | tf_op jit(solution)/shard_map/hbk,khe->bhe/dot_general | solution.py:127
  67.9 17.2 %all-gather.6.cloned.1.call-done = bf16[704,768]{0,1:T(8,128)(2,1)} async-done(((bf16[704,192]{0,1:T(8,128)(2,1)}), bf16[704,768]{0,1:T(8,128)(2,1)}) %all-gather.6.cloned.1.call-update) | async-done | bytes 1081360 | tf_op jit(solution)/shard_map/all_gather | solution.py:59
  85.1 19.6 %all-gather.8.cloned.1.call-done = bf16[768,768]{1,0:T(8,128)(2,1)} async-done(((bf16[192,768]{1,0:T(8,128)(2,1)}), bf16[768,768]{1,0:T(8,128)(2,1)}) %all-gather.8.cloned.1.call-update) | async-done | bytes 1179664 | tf_op jit(solution)/shard_map/all_gather | solution.py:59
  104.7 3.6 fusion.156
  108.7 1.1 fusion.88
  109.9 1.3 copy-done.39
  111.2 2.4 convolution_convert_fusion.5
  114.5 35.7 %all-reduce.10.cloned.1.call-done = bf16[704,768]{1,0:T(8,128)(2,1)} async-done(((bf16[704,768]{1,0:T(8,128)(2,1)}), bf16[704,768]{1,0:T(8,128)(2,1)}) %all-reduce.10.cloned.1.call-update) | async-done | bytes 1081360 | tf_op jit(solution)/shard_map/psum | solution.py:135
  150.2 1.5 fusion.152
  153.3 1.1 fusion.157
  154.5 1.6 select_reduce_fusion
  157.6 22.0 %psum.106 = f32[]{:T(128)} all-reduce(f32[]{:T(128)} %get-tuple-element.38), channel_id=1, replica_groups=mesh['tables'=8,'heads'=4] {'tables'}, use_global_device_ids=true, to_apply=%region_14.15 | all-reduce | flops 1 | bytes 8 | tf_op jit(solution)/shard_map/psum | solution.py:108
  180.3 2.8 multiply_reduce_fusion.4
  184.7 1.4 copy-done.40
  186.2 2.3 fusion.53
  189.4 2.0 convolution_convert_fusion.4
  191.5 3.6 convolution_convert_fusion.3
  195.1 1.9 fusion.135
  197.1 4.7 convolution_convert_fusion.2
  201.8 9.3 %all-reduce.16.cloned.1.call-start = ((), (), s32[]{:S(2)}) async-start(), calls=%async_computation.5 | async-start | bytes 1032192 | tf_op jit(solution)/shard_map/psum | solution.py:201
  211.2 17.2 %all-reduce.12.cloned.1.call-done = bf16[704,768]{1,0:T(8,128)(2,1)} async-done(((bf16[704,768]{1,0:T(8,128)(2,1)}), bf16[704,768]{1,0:T(8,128)(2,1)}) %all-reduce.12.cloned.1.call-update) | async-done | bytes 1081360 | tf_op jit(solution)/shard_map/psum | solution.py:155
  228.4 1.9 fusion.45
  230.3 1.2 fusion.46
  232.8 1.3 copy-done.5
  234.9 8.7 %fusion.31 = bf16[3,64,2048]{2,1,0:T(8,128)(2,1)} fusion(bf16[704,3,64]{0,2,1:T(8,128)(2,1)S(1)} %bitcast.101, f32[3,704,2048]{2,1,0:T(8,128)} %get-tuple-element.92, f32[3,704]{1,0:T(4,128)S(1)} %copy-done.73), kind=kOutput, calls=%fused_computation.48 | convolution fusion | flops 562692096 | bytes 18366720 | tf_op jit(solution)/shard_map/hbk,bhe->khe/dot_general | solution.py:162
  243.5 8.4 %fusion.158 = f32[3,704,2048]{2,1,0:T(8,128)} fusion(bf16[704,3,64]{0,2,1:T(8,128)(2,1)S(1)} %bitcast.102, bf16[2048,3,64]{0,2,1:T(8,128)(2,1)S(1)} %bitcast.94), kind=kOutput, calls=%fused_computation.241 | convolution fusion | flops 553648128 | bytes 18358272 | tf_op jit(solution)/shard_map/bhe,khe->hbk/dot_general | solution.py:165
  251.9 29.1 %fusion.63 = bf16[3,64,704]{2,1,0:T(8,128)(2,1)} fusion(bf16[2048,3,64]{0,2,1:T(8,128)(2,1)S(1)} %bitcast.106, f32[3,704,2048]{2,1,0:T(8,128)} %fusion.158, f32[3,704,2048]{2,1,0:T(8,128)} %get-tuple-element.92, f32[3,704]{1,0:T(4,128)S(1)} %copy-done.73), kind=kOutput, calls=%fused_computation.100 | convolution fusion | flops 597041216 | bytes 35668224 | tf_op jit(solution)/shard_map/hbk,khe->bhe/dot_general | solution.py:170
  281.0 26.8 %fusion.34 = bf16[3,64,2048]{2,1,0:T(8,128)(2,1)} fusion(bf16[704,3,64]{0,2,1:T(8,128)(2,1)} %bitcast.113, f32[3,704,2048]{2,1,0:T(8,128)} %fusion.158, f32[3,704,2048]{2,1,0:T(8,128)} %get-tuple-element.92, f32[3,704]{1,0:T(4,128)S(1)} %copy-done.73), kind=kOutput, calls=%fused_computation.49 | convolution fusion | flops 597299264 | bytes 35668224 | tf_op jit(solution)/shard_map/hbk,bhe->khe/dot_general | solution.py:171
  307.8 3.2 fusion.72
  311.0 1.0 fusion.99
  312.1 1.9 fusion.73
  314.1 5.5 multiply_reduce_fusion.1
  319.6 2.6 fusion.150
  322.2 1.1 fusion.69
  323.4 2.2 fusion.68
  328.2 1.4 fusion.70
  329.6 1.4 fusion.71
  330.9 2.1 pad_maximum_fusion
  333.1 1.1 convolution_convert_fusion.9
  334.4 1.6 multiply_reduce_fusion.12
  336.0 39.8 %psum.115 = f32[1,768]{1,0:T(1,128)S(1)} all-reduce(f32[1,768]{1,0:T(1,128)S(1)} %stack.32), channel_id=1, replica_groups=mesh['tables'=8,'heads'=4] {'tables','heads'}, use_global_device_ids=true, to_apply=%region_40.41 | all-reduce | flops 768 | bytes 6144 | tf_op jit(solution)/shard_map/psum | solution.py:201
  375.8 22.0 %all-reduce.2 = (f32[1,768]{1,0:T(1,128)S(1)}, f32[1,768]{1,0:T(1,128)S(1)}, f32[]{:T(128)}) all-reduce(f32[1,768]{1,0:T(1,128)S(1)} %stack.34, f32[1,768]{1,0:T(1,128)S(1)} %stack.33, f32[]{:T(128)} %get-tuple-element.37), channel_id=1, replica_groups=mesh['tables'=8,'heads'=4] {'tables'}, use_global_device_ids=true, to_apply=%region_44.45 | all-reduce | flops 1537 | bytes 12296 | tf_op jit(solution)/shard_map/psum | solution.py:204
  398.4 63.3 %all-reduce.16.cloned.1.call-done = (f32[100,768]{1,0:T(8,128)}, f32[64,768]{1,0:T(8,128)}) async-done(((f32[100,768]{1,0:T(8,128)}, f32[64,768]{1,0:T(8,128)}), (f32[100,768]{1,0:T(8,128)}, f32[64,768]{1,0:T(8,128)})) %all-reduce.16.cloned.1.call-update) | async-done | bytes 503824 | tf_op jit(solution)/shard_map/psum | solution.py:201
  461.7 1.7 multiply_reduce_fusion.13
  463.4 1.7 multiply_reduce_fusion.11
  467.0 140.0 %all-reduce.18.cloned.1.call-done = (bf16[3,768,192]{1,2,0:T(8,128)(2,1)}, bf16[192,768]{1,0:T(8,128)(2,1)}, bf16[768,768]{1,0:T(8,128)(2,1)}, bf16[768,768]{1,0:T(8,128)(2,1)}) async-done(((bf16[3,768,192]{1,2,0:T(8,128)(2,1)}, bf16[192,768]{1,0:T(8,128)(2,1)}, bf16[768,768]{1,0:T(8,128)(2,1)}, bf16[768,768]{1,0:T(8,128)(2,1)}), (bf16[3,768,192]{1,2,0:T(8,128)(2,1)}, bf16[192,768]{1,0:T(8,128)(2,1)}, ...) | async-done | bytes 3538960 | tf_op jit(solution)/shard_map/psum | solution.py:197
  607.0 1.7 fusion.80
  608.8 2.3 fusion.58
  612.3 2.8 fusion.41
  617.2 7.6 %psum.113 = f32[]{:T(128)} all-reduce(f32[]{:T(128)S(6)} %add.280), channel_id=1, replica_groups=mesh['tables'=8,'heads'=4] {'heads'}, use_global_device_ids=true, to_apply=%region_34.35 | all-reduce | flops 1 | bytes 8 | tf_op jit(solution)/shard_map/psum | solution.py:220
  627.2 2.3 multiply_subtract_fusion.3
  629.5 3.0 add_subtract_fusion
  632.5 3.3 multiply_subtract_fusion.2
  635.9 1.3 copy-done.35
  637.9 4.4 multiply_subtract_fusion
  643.8 4.1 multiply_subtract_fusion.1
  (221 shorter events, 27.8 us)
Async XLA Ops:
  7.2 24.7 %copy-start.27 = (f32[100,768]{1,0:T(8,128)S(1)}, f32[100,768]{1,0:T(8,128)}, u32[]{:S(2)}) copy-start(f32[100,768]{1,0:T(8,128)} %param.36) | copy-start | bytes 921604
  7.2 77.8 %all-gather.6.cloned.1.call-start = ((), (), s32[]{:S(2)}) async-start(), calls=%async_computation | async-start | bytes 1474560 | tf_op jit(solution)/shard_map/all_gather | solution.py:59
  23.7 9.3 %copy-start.61 = (s32[1,4,4,128]{3,1,2,0:T(4,128)}, s32[1,4,4,128]{3,1,2,0:T(4,128)S(1)}, u32[]{:S(2)}) copy-start(s32[1,4,4,128]{3,1,2,0:T(4,128)S(1)} %copy.57) | copy-start | bytes 24580
  30.2 2.8 copy-start.18
  31.9 15.1 %copy-start.16 = (bf16[3,768,192]{1,2,0:T(8,128)(2,1)}, bf16[3,768,192]{1,2,0:T(8,128)(2,1)S(1)}, u32[]{:S(2)}) copy-start(bf16[3,768,192]{1,2,0:T(8,128)(2,1)S(1)} %convert_element_type.168) | copy-start | bytes 2654212
  34.2 2.6 copy-start
  37.6 1.7 copy-start.7
  38.4 10.1 %copy-start.51 = (bf16[2048,192]{0,1:T(8,128)(2,1)}, bf16[2048,192]{0,1:T(8,128)(2,1)S(1)}, u32[]{:S(2)}) copy-start(bf16[2048,192]{0,1:T(8,128)(2,1)S(1)} %convolution_convert_fusion.1) | copy-start | bytes 2359300
  39.3 18.0 %copy-start.25 = (bf16[2048,192]{0,1:T(8,128)(2,1)}, bf16[2048,192]{0,1:T(8,128)(2,1)S(1)}, u32[]{:S(2)}) copy-start(bf16[2048,192]{0,1:T(8,128)(2,1)S(1)} %convolution_convert_fusion) | copy-start | bytes 2359300
  48.5 8.8 %copy-start.70 = (bf16[704,192]{0,1:T(8,128)(2,1)}, bf16[704,192]{0,1:T(8,128)(2,1)S(1)}, u32[]{:S(2)}) copy-start(bf16[704,192]{0,1:T(8,128)(2,1)S(1)} %convolution_convert_fusion.11) | copy-start | bytes 811012
  57.3 9.4 %copy-start.72 = (f32[3,704]{1,0:T(4,128)}, f32[3,704]{1,0:T(4,128)S(1)}, u32[]{:S(2)}) copy-start(f32[3,704]{1,0:T(4,128)S(1)} %get-tuple-element.91) | copy-start | bytes 25348
  57.3 9.5 %copy-start.30 = (f32[192,768]{1,0:T(8,128)S(1)}, f32[192,768]{1,0:T(8,128)}, u32[]{:S(2)}) copy-start(f32[192,768]{1,0:T(8,128)} %param.40) | copy-start | bytes 1769476
  66.8 37.9 %all-gather.8.cloned.1.call-start = ((), (), s32[]{:S(2)}) async-start(), calls=%async_computation.1 | async-start | bytes 1474560 | tf_op jit(solution)/shard_map/all_gather | solution.py:59
  67.6 82.6 %all-reduce.10.cloned.1.call-start = ((), (), s32[]{:S(2)}) async-start(), calls=%async_computation.2 | async-start | bytes 2162688 | tf_op jit(solution)/shard_map/psum | solution.py:135
  104.7 4.0 copy-start.10
  108.7 2.5 copy-start.32
  113.6 114.7 %all-reduce.12.cloned.1.call-start = ((), (), s32[]{:S(2)}) async-start(), calls=%async_computation.3 | async-start | bytes 2162688 | tf_op jit(solution)/shard_map/psum | solution.py:155
  180.2 2.8 copy-start.4
  183.1 1.7 copy-start.33
  183.1 3.1 copy-start.40
  183.9 4.5 copy-start.13
  186.2 3.3 copy-start.11
  195.1 139.3 %all-reduce.14.cloned.1.call-start = ((), (), s32[]{:S(2)}) async-start(), calls=%async_computation.4 | async-start | bytes 393216 | tf_op jit(solution)/shard_map/psum | solution.py:204
  201.8 259.9 %all-reduce.16.cloned.1.call-start = ((), (), s32[]{:S(2)}) async-start(), calls=%async_computation.5 | async-start | bytes 1032192 | tf_op jit(solution)/shard_map/psum | solution.py:201
  228.4 1.9 copy-start.9
  230.2 1.6 copy-start.14
  231.8 2.3 copy-start.29
  234.9 8.7 %copy-start.26 = (bf16[2048,192]{0,1:T(8,128)(2,1)S(1)}, bf16[2048,192]{0,1:T(8,128)(2,1)}, u32[]{:S(2)}) copy-start(bf16[2048,192]{0,1:T(8,128)(2,1)} %copy-done.25) | copy-start | bytes 2359300
  243.5 8.4 %copy-start.52 = (bf16[2048,192]{0,1:T(8,128)(2,1)S(1)}, bf16[2048,192]{0,1:T(8,128)(2,1)}, u32[]{:S(2)}) copy-start(bf16[2048,192]{0,1:T(8,128)(2,1)} %copy-done.51) | copy-start | bytes 2359300
  281.0 26.8 %copy-start.8 = (bf16[2048,768]{0,1:T(8,128)(2,1)S(1)}, bf16[2048,768]{0,1:T(8,128)(2,1)}, u32[]{:S(2)}) copy-start(bf16[2048,768]{0,1:T(8,128)(2,1)} %copy-done.7) | copy-start | bytes 9437188
  307.8 3.2 copy-start.17
  307.8 3.2 copy-start.42
  312.1 7.4 %slice-start = ((s8[6291456]{0:T(1024)(128)(4,1)}), s8[4194304]{0:T(1024)(128)(4,1)S(1)}, s32[]{:S(2)}) async-start(s8[6291456]{0:T(1024)(128)(4,1)} %bitcast.91), calls=%async_computation.7 | async-start | bytes 8388608
  314.0 5.5 slice-start.1
  319.6 2.6 copy-start.19
  323.4 2.3 copy-start.2
  323.4 2.3 copy-start.48
  330.9 2.2 copy-start.49
  333.1 274.0 %all-reduce.18.cloned.1.call-start = ((), (), s32[]{:S(2)}) async-start(), calls=%async_computation.6 | async-start | bytes 7077888 | tf_op jit(solution)/shard_map/psum | solution.py:197
  334.3 291.3 %copy-start.64 = (f32[3,768]{1,0:T(4,128)S(1)}, f32[3,768]{1,0:T(4,128)}, u32[]{:S(2)}) copy-start(f32[3,768]{1,0:T(4,128)} %param.38) | copy-start | bytes 27652
  334.3 291.3 %copy-start.67 = (f32[3,768]{1,0:T(4,128)S(1)}, f32[3,768]{1,0:T(4,128)}, u32[]{:S(2)}) copy-start(f32[3,768]{1,0:T(4,128)} %param.46) | copy-start | bytes 27652
  334.3 291.3 %copy-start.68 = (f32[3,768]{1,0:T(4,128)S(1)}, f32[3,768]{1,0:T(4,128)}, u32[]{:S(2)}) copy-start(f32[3,768]{1,0:T(4,128)} %param.54) | copy-start | bytes 27652
  335.9 290.3 %copy-start.56 = (f32[64,768]{1,0:T(8,128)S(1)}, f32[64,768]{1,0:T(8,128)}, u32[]{:S(2)}) copy-start(f32[64,768]{1,0:T(8,128)} %param.37) | copy-start | bytes 589828
  335.9 290.3 %copy-start.57 = (f32[64,768]{1,0:T(8,128)S(1)}, f32[64,768]{1,0:T(8,128)}, u32[]{:S(2)}) copy-start(f32[64,768]{1,0:T(8,128)} %param.45) | copy-start | bytes 589828
  335.9 290.3 %copy-start.58 = (f32[64,768]{1,0:T(8,128)S(1)}, f32[64,768]{1,0:T(8,128)}, u32[]{:S(2)}) copy-start(f32[64,768]{1,0:T(8,128)} %param.53) | copy-start | bytes 589828
  461.7 164.5 %copy-start.54 = (f32[64,768]{1,0:T(8,128)S(1)}, f32[64,768]{1,0:T(8,128)}, u32[]{:S(2)}) copy-start(f32[64,768]{1,0:T(8,128)} %get-tuple-element.43) | copy-start | bytes 589828
  608.7 18.4 %copy-start.28 = (f32[100,768]{1,0:T(8,128)S(1)}, f32[100,768]{1,0:T(8,128)}, u32[]{:S(2)}) copy-start(f32[100,768]{1,0:T(8,128)} %param.36) | copy-start | bytes 921604
  608.7 18.4 %copy-start.47 = (f32[100,768]{1,0:T(8,128)S(1)}, f32[100,768]{1,0:T(8,128)}, u32[]{:S(2)}) copy-start(f32[100,768]{1,0:T(8,128)} %get-tuple-element.42) | copy-start | bytes 921604
  615.2 14.3 %copy-start.31 = (f32[192,768]{1,0:T(8,128)S(1)}, f32[192,768]{1,0:T(8,128)}, u32[]{:S(2)}) copy-start(f32[192,768]{1,0:T(8,128)} %param.40) | copy-start | bytes 1769476
  626.2 6.2 copy-start.44
  627.2 5.3 copy-start.43
  629.5 3.0 copy-start.15
  629.5 3.0 copy-start.24
  632.5 3.4 copy-start.21
  632.5 3.4 copy-start.34
  632.5 4.6 copy-start.35
  632.5 5.3 copy-start.36
  637.9 4.4 copy-start.12
  637.9 4.4 copy-start.20
  637.9 5.1 copy-start.37
  637.9 6.0 copy-start.38
  643.8 4.2 copy-start.53
  643.8 4.2 copy-start.59
  643.8 4.2 copy-start.60
  (19 other events, 23.3 us)
Sparse Core Ops, SparseCore 0:
  66.9 18.1 all-gather.5
  87.2 17.4 all-gather.7
  113.8 36.3 all-reduce.9
  195.2 33.0 all-reduce.11
  232.1 70.4 all-reduce.13
  333.2 128.5 all-reduce.15
  467.4 139.5 all-reduce.17

commit v2 on v1

--- a/solution.py
+++ b/solution.py
@@ -1,6 +1,8 @@
 import jax
 import jax.numpy as jnp
 from jax import lax
+from jax.experimental import pallas as pl
+from jax.experimental.pallas import tpu as pltpu
 from jax.sharding import PartitionSpec as P
 
 HD = 64
@@ -19,6 +21,7 @@
 MASKED = -1e30
 FLOAT = jnp.float32
 HALF = jnp.bfloat16
+MESH = pl.DeviceIdType.MESH
 
 
 def product(left, right):
@@ -57,6 +60,331 @@
 
 def gather(rows, axis=0):
     return lax.all_gather(rows, "heads", axis=axis, tiled=True)
+
+
+def place_bit(place, bit):
+    return lax.rem(lax.div(place, bit), 2)
+
+
+def bits_of(size):
+    return [1 << power for power in range(size.bit_length() - 1)]
+
+
+class Pool:
+    def __init__(self, send_sems, recv_sems, landing):
+        self.send_sems, self.recv_sems, self.landing = send_sems, recv_sems, landing
+        self.copies = self.rows = 0
+
+    def semaphores(self):
+        self.copies += 1
+        return self.send_sems.at[self.copies - 1], self.recv_sems.at[self.copies - 1]
+
+    def land(self, rows):
+        self.rows += rows
+        return self.landing.at[pl.ds(self.rows - rows, rows), :]
+
+
+def stages_of(rows, axes, least):
+    steps = []
+    for axis, bit in axes:
+        if rows // 2 >= least and rows % 32 == 0:
+            rows //= 2
+            steps.append((axis, bit, "halve", rows))
+        else:
+            steps.append((axis, bit, "whole", rows))
+    back = [(axis, bit, "back", left) for axis, bit, kind, left in reversed(steps) if kind == "halve"]
+    return steps + back
+
+
+def landing_rows(steps):
+    return sum(left for _, _, kind, left in steps if kind != "back")
+
+
+class Sum:
+    def __init__(self, pool, buffer, result, start, steps, places):
+        self.pool, self.buffer, self.result, self.low = pool, buffer, result, start
+        self.steps, self.places = steps, places
+        self.at, self.copy, self.landed = 0, None, None
+
+    def rows(self, low, count):
+        return pl.ds(pl.multiple_of(low, 16), count)
+
+    def finish(self):
+        if self.copy is None:
+            return
+        _, _, kind, count = self.steps[self.at - 1]
+        self.copy.wait()
+        self.copy = None
+        if kind != "back":
+            mine = self.rows(self.low, count)
+            total = self.buffer[mine, :].astype(FLOAT) + self.landed[...].astype(FLOAT)
+            last = self.at == len(self.steps) or self.steps[self.at][2] == "back"
+            target = self.result if last else self.buffer
+            target[mine, :] = total.astype(self.buffer.dtype)
+
+    def start(self):
+        if self.at >= len(self.steps):
+            return
+        axis, bit, kind, count = self.steps[self.at]
+        self.at += 1
+        side = place_bit(self.places[axis], bit)
+        other = dict(self.places)
+        other[axis] = self.places[axis] + bit - 2 * bit * side
+        if kind == "halve":
+            source = self.buffer.at[self.rows(self.low + count * (1 - side), count), :]
+            self.low = self.low + count * side
+            self.landed = self.pool.land(count)
+            target = self.landed
+        elif kind == "whole":
+            source = self.buffer.at[self.rows(self.low, count), :]
+            self.landed = self.pool.land(count)
+            target = self.landed
+        else:
+            source = target = self.result.at[self.rows(self.low, count), :]
+            self.low = self.low - count * side
+        send_sem, recv_sem = self.pool.semaphores()
+        self.copy = pltpu.make_async_remote_copy(
+            src_ref=source,
+            dst_ref=target,
+            send_sem=send_sem,
+            recv_sem=recv_sem,
+            device_id=(other["tables"], other["heads"]),
+            device_id_type=MESH,
+        )
+        self.copy.start()
+
+    def advance(self):
+        self.finish()
+        self.start()
+
+    def done(self):
+        return self.at >= len(self.steps) and self.copy is None
+
+
+def places_here():
+    return {"tables": lax.axis_index("tables"), "heads": lax.axis_index("heads")}
+
+
+def greet(places, axes):
+    barrier = pltpu.get_barrier_semaphore()
+    for axis, bit in axes:
+        other = dict(places)
+        other[axis] = places[axis] + bit - 2 * bit * place_bit(places[axis], bit)
+        pl.semaphore_signal(
+            barrier, inc=1, device_id=(other["tables"], other["heads"]), device_id_type=MESH
+        )
+    pl.semaphore_wait(barrier, len(axes))
+
+
+SMALL = {"head": (0, 64), "bins": (64, 64), "embed": (128, 112), "gains": (240, 16)}
+SMALL_ROWS = 256
+
+
+def reduce_plan(sizes, main_rows):
+    over_tables = [("tables", bit) for bit in bits_of(sizes["tables"])]
+    over_heads = [("heads", bit) for bit in bits_of(sizes["heads"])]
+    chunk = 384 if main_rows % 384 == 0 else main_rows
+    main = [stages_of(chunk, over_tables, 16) for _ in range(main_rows // chunk)]
+    small = stages_of(SMALL_ROWS, over_heads + over_tables, 64)
+    return over_tables, over_heads, chunk, main, small
+
+
+def sum_squares(rows_ref, count):
+    def piece(step, total):
+        part = rows_ref[pl.ds(pl.multiple_of(step * 64, 64), 64), :].astype(FLOAT)
+        return total + jnp.sum((part * part).reshape(8, 8, part.shape[1]), axis=0)
+
+    return lax.fori_loop(0, count // 64, piece, jnp.zeros((8, rows_ref.shape[1]), FLOAT))
+
+
+def one_value(total):
+    value = jnp.sum(jnp.sum(total, axis=0, keepdims=True), axis=1, keepdims=True)
+    return jnp.broadcast_to(value, (8, 128))
+
+
+def reduce_kernel(sizes, in_refs, out_refs, scratch):
+    down, up, out, qkv, small, loss = in_refs
+    main_ref, small_ref, stats_ref = out_refs
+    main_work, small_work, loss_work, square_work, landing, loss_buf, square_buf, loss_land, square_land, sends, recvs = scratch
+    places = places_here()
+    over_tables, over_heads, chunk, main_steps, small_steps = reduce_plan(sizes, main_ref.shape[0])
+    greet(places, over_tables + over_heads)
+    low = 0
+    for part in (down, up, out, qkv):
+        main_work[pl.ds(low, part.shape[0]), :] = part[...]
+        low += part.shape[0]
+    small_work[...] = small[...]
+    loss_work[...] = loss[...]
+    pool = Pool(sends, recvs, landing)
+    mains = [
+        Sum(pool, main_work, main_ref, chunk * place, steps, places) for place, steps in enumerate(main_steps)
+    ]
+    smalls = Sum(pool, small_work, small_ref, 0, small_steps, places)
+    losses = Sum(
+        Pool(sends.at[pl.ds(64, 16)], recvs.at[pl.ds(64, 16)], loss_land),
+        loss_work,
+        loss_buf,
+        0,
+        stages_of(16, over_heads + over_tables, 16),
+        places,
+    )
+    waiting = len(over_heads)
+    slots = len(mains) - 1 + len(main_steps[0]) + 1
+    for slot in range(slots):
+        for place, part in enumerate(mains):
+            if 0 <= slot - place <= len(part.steps):
+                part.advance()
+        if smalls.at < len(small_steps) - waiting:
+            smalls.advance()
+        losses.advance()
+    while smalls.at < len(small_steps) - waiting:
+        smalls.advance()
+    while not losses.done():
+        losses.advance()
+    square_work[...] = jnp.broadcast_to(
+        one_value(sum_squares(main_ref, main_ref.shape[0]))[:1], square_work.shape
+    )
+    squares = Sum(
+        Pool(sends.at[pl.ds(80, 8)], recvs.at[pl.ds(80, 8)], square_land),
+        square_work,
+        square_buf,
+        0,
+        stages_of(16, list(reversed(over_heads)), 16),
+        places,
+    )
+    while not (squares.done() and smalls.done()):
+        smalls.advance()
+        squares.advance()
+    whole = one_value(sum_squares(small_ref, SMALL_ROWS))
+    row = lax.broadcasted_iota(jnp.int32, (8, 128), 0)
+    stats_ref[...] = jnp.where(row == 0, square_buf[:8] + whole, loss_buf[:8])
+
+
+def reduce_gradients(sizes, down, up, out, qkv, small, loss):
+    main_rows = down.shape[0] + up.shape[0] + out.shape[0] + qkv.shape[0]
+    width = down.shape[1]
+    over_tables, over_heads, chunk, main_steps, small_steps = reduce_plan(sizes, main_rows)
+    rows = sum(map(landing_rows, main_steps)) + landing_rows(small_steps)
+    tiny = 16 * (len(over_tables) + len(over_heads))
+    whole = pl.BlockSpec(memory_space=pltpu.VMEM)
+    assert sum(map(len, main_steps)) + len(small_steps) <= 64 or sizes["tables"] > 8
+
+    def kernel(*refs):
+        reduce_kernel(sizes, refs[:6], refs[6:9], refs[9:])
+
+    return pl.pallas_call(
+        kernel,
+        out_shape=(
+            jax.ShapeDtypeStruct((main_rows, width), HALF),
+            jax.ShapeDtypeStruct((SMALL_ROWS, width), HALF),
+            jax.ShapeDtypeStruct((8, 128), FLOAT),
+        ),
+        in_specs=[whole] * 6,
+        out_specs=(whole,) * 3,
+        scratch_shapes=[
+            pltpu.VMEM((main_rows, width), HALF),
+            pltpu.VMEM((SMALL_ROWS, width), HALF),
+            pltpu.VMEM((16, 128), FLOAT),
+            pltpu.VMEM((16, 128), FLOAT),
+            pltpu.VMEM((rows, width), HALF),
+            pltpu.VMEM((16, 128), FLOAT),
+            pltpu.VMEM((16, 128), FLOAT),
+            pltpu.VMEM((tiny, 128), FLOAT),
+            pltpu.VMEM((16 * len(over_heads), 128), FLOAT),
+            pltpu.SemaphoreType.DMA((160,)),
+            pltpu.SemaphoreType.DMA((160,)),
+        ],
+        compiler_params=pltpu.CompilerParams(
+            collective_id=1, has_side_effects=True, vmem_limit_bytes=32 * 2**20
+        ),
+        name="reduce_gradients",
+    )(down, up, out, qkv, small, loss)
+
+
+def adam_kernel(refs):
+    (stats, main_d, main_u, main_o, main_q, small) = refs[:6]
+    w = refs[6:14]
+    m = refs[14:22]
+    v = refs[22:30]
+    w_new = refs[30:38]
+    m_new = refs[38:46]
+    v_new = refs[46:54]
+    norm_ref = refs[54]
+    norm = jnp.sqrt(stats[0:1, 0:1])
+    norm_ref[...] = jnp.broadcast_to(norm, norm_ref.shape)
+    factor = jnp.minimum(1.0, CLIP_NORM / (norm + 1e-06))
+
+    def update(which, gradient, rate, decay, at=...):
+        gradient = gradient.astype(FLOAT) * factor
+        results = adam_update(w[which][at], m[which][at], v[which][at], gradient, rate, decay)
+        for target, value in zip((w_new, m_new, v_new), results):
+            target[which][at] = value
+
+    update(6, main_d[...], RATE, DECAY)
+    update(5, main_u[...], RATE, DECAY)
+    update(4, main_o[...], RATE_WIDE, DECAY)
+    width = w[3].shape[2]
+    turned = main_q[...].astype(FLOAT).T
+    for part in range(3):
+        update(3, turned[:, part * width : (part + 1) * width], RATE, DECAY, at=part)
+
+    @pl.when(pl.program_id(0) == 0)
+    def _():
+        def rows(name, count):
+            low, size = SMALL[name]
+            return small[low : low + size, :].astype(FLOAT)[:count]
+
+        update(0, rows("embed", w[0].shape[0]), RATE, DECAY)
+        update(1, rows("bins", w[1].shape[0]), RATE_WIDE, DECAY)
+        update(2, rows("gains", w[2].shape[0]), RATE_WIDE, 0.0)
+        update(7, rows("head", w[7].shape[1]).T, RATE, DECAY)
+
+
+def adam_all(stats, main, small, weights, firsts, seconds):
+    width = main.shape[1]
+    steps = width // 128
+    hidden = weights[5].shape[1]
+    inner = weights[4].shape[0]
+    low_out, low_qkv = 2 * hidden, 2 * hidden + inner
+
+    def fixed(array):
+        return pl.BlockSpec(array.shape, lambda step: (0,) * array.ndim)
+
+    def rows_of(array):
+        return pl.BlockSpec((array.shape[0] // steps, array.shape[1]), lambda step: (step, 0))
+
+    blocks = [
+        fixed(weights[0]),
+        fixed(weights[1]),
+        fixed(weights[2]),
+        pl.BlockSpec((3, width // steps, inner), lambda step: (0, step, 0)),
+        rows_of(weights[4]),
+        rows_of(weights[5]),
+        rows_of(weights[6]),
+        fixed(weights[7]),
+    ]
+    down = main[:hidden]
+    up = main[hidden:low_out]
+    out = main[low_out:low_qkv]
+    qkv = main[low_qkv:]
+    shapes = [jax.ShapeDtypeStruct(weight.shape, FLOAT) for weight in weights]
+    return pl.pallas_call(
+        lambda *refs: adam_kernel(refs),
+        grid=(steps,),
+        in_specs=[
+            fixed(stats),
+            rows_of(down),
+            rows_of(up),
+            rows_of(out),
+            pl.BlockSpec((qkv.shape[0], width // steps), lambda step: (0, step)),
+            fixed(small),
+        ]
+        + blocks * 3,
+        out_specs=blocks * 3 + [fixed(stats)],
+        out_shape=shapes * 3 + [jax.ShapeDtypeStruct(stats.shape, FLOAT)],
+        compiler_params=pltpu.CompilerParams(vmem_limit_bytes=48 * 2**20),
+        name="adam",
+    )(stats, down, up, out, qkv, small, *weights, *firsts, *seconds)
 
 
 def shards(
@@ -172,11 +500,11 @@
     back_query = back_query.reshape(total_qry, -1).astype(HALF)
     back_key = back_key.reshape(total_ctx, -1).astype(HALF)
     back_value = back_value.reshape(total_ctx, -1).astype(HALF)
-    grad_qkv = jnp.stack(
+    grad_qkv = jnp.concatenate(
         [
-            jnp.einsum("rd,rc->dc", normed_qry, back_query, preferred_element_type=FLOAT),
-            jnp.einsum("rd,rc->dc", normed_ctx, back_key, preferred_element_type=FLOAT),
-            jnp.einsum("rd,rc->dc", normed_ctx, back_value, preferred_element_type=FLOAT),
+            jnp.einsum("rc,rd->cd", back_query, normed_qry, preferred_element_type=FLOAT),
+            jnp.einsum("rc,rd->cd", back_key, normed_ctx, preferred_element_type=FLOAT),
+            jnp.einsum("rc,rd->cd", back_value, normed_ctx, preferred_element_type=FLOAT),
         ]
     )
     part_qry = jnp.einsum("rc,dc->rd", back_query, qkv_half[0], preferred_element_type=FLOAT)
@@ -192,84 +520,38 @@
         "rx,rd->xd", qry_rows, back_qry, preferred_element_type=FLOAT
     ) + jnp.einsum("rx,rd->xd", ctx_rows, back_ctx, preferred_element_type=FLOAT)
     grad_bins = jnp.einsum("rb,rd->bd", bin_hits, back_ctx, preferred_element_type=FLOAT)
-    grad_qkv, grad_out, grad_up, grad_down = [
-        total.astype(FLOAT)
-        for total in lax.psum(
-            tuple(part.astype(HALF) for part in (grad_qkv, grad_out, grad_up, grad_down)), "tables"
-        )
-    ]
-    grad_embed, grad_bins, grad_first = lax.psum(
-        (grad_embed, grad_bins, gain_qry + gain_ctx), ("tables", "heads")
-    )
-    grad_head, grad_mid, grad_final, loss_sum = lax.psum(
-        (grad_head, grad_mid, grad_final, loss_local), "tables"
-    )
-    grad_gains = jnp.stack([grad_first, grad_mid, grad_final])
-    split_squares = (
-        jnp.sum(grad_qkv * grad_qkv)
-        + jnp.sum(grad_out * grad_out)
-        + jnp.sum(grad_up * grad_up)
-        + jnp.sum(grad_down * grad_down)
-    )
-    whole_squares = (
-        jnp.sum(grad_embed * grad_embed)
-        + jnp.sum(grad_bins * grad_bins)
-        + jnp.sum(grad_gains * grad_gains)
-        + jnp.sum(grad_head * grad_head)
-    )
-    grad_norm = jnp.sqrt(lax.psum(split_squares, "heads") + whole_squares)
-    factor = jnp.minimum(1.0, CLIP_NORM / (grad_norm + 1e-06))
-    embed_new, embed_first, embed_second = adam_update(
-        w_embed, m_embed, v_embed, grad_embed * factor, RATE, DECAY
-    )
-    bins_new, bins_first, bins_second = adam_update(
-        w_bins, m_bins, v_bins, grad_bins * factor, RATE_WIDE, DECAY
-    )
-    gains_new, gains_first, gains_second = adam_update(
-        norm_gains, m_gains, v_gains, grad_gains * factor, RATE_WIDE, 0.0
-    )
-    qkv_new, qkv_first, qkv_second = adam_update(
-        w_qkv, m_qkv, v_qkv, grad_qkv * factor, RATE, DECAY
-    )
-    out_new, out_first, out_second = adam_update(
-        w_out, m_out, v_out, grad_out * factor, RATE_WIDE, DECAY
-    )
-    up_new, up_first, up_second = adam_update(w_up, m_up, v_up, grad_up * factor, RATE, DECAY)
-    down_new, down_first, down_second = adam_update(
-        w_down, m_down, v_down, grad_down * factor, RATE, DECAY
-    )
-    head_new, head_first, head_second = adam_update(
-        w_head, m_head, v_head, grad_head * factor, RATE, DECAY
-    )
-    return (
-        embed_new,
-        bins_new,
-        gains_new,
-        qkv_new,
-        out_new,
-        up_new,
-        down_new,
-        head_new,
-        embed_first,
-        bins_first,
-        gains_first,
-        qkv_first,
-        out_first,
-        up_first,
-        down_first,
-        head_first,
-        embed_second,
-        bins_second,
-        gains_second,
-        qkv_second,
-        out_second,
-        up_second,
-        down_second,
-        head_second,
-        loss_sum,
-        query_count,
-        grad_norm,
-    )
+    groups = lax.axis_size("heads")
+    sizes = {"tables": lax.axis_size("tables"), "heads": groups}
+    grad_head = jnp.transpose(grad_head) / groups
+    gains = jnp.stack([gain_qry + gain_ctx, grad_mid / groups, grad_final / groups])
+    feature_pad = SMALL["embed"][1] - grad_embed.shape[0]
+    gains_pad = SMALL["gains"][1] - gains.shape[0]
+    small = jnp.concatenate(
+        [
+            grad_head,
+            grad_bins,
+            jnp.pad(grad_embed, ((0, feature_pad), (0, 0))),
+            jnp.pad(gains, ((0, gains_pad), (0, 0))),
+        ]
+    ).astype(HALF)
+    main, small, stats = reduce_gradients(
+        sizes,
+        grad_down.astype(HALF),
+        grad_up.astype(HALF),
+        grad_out.astype(HALF),
+        grad_qkv.astype(HALF),
+        small,
+        jnp.full((16, 128), loss_local / groups, FLOAT),
+    )
+    results = adam_all(
+        stats,
+        main,
+        small,
+        (w_embed, w_bins, norm_gains, w_qkv, w_out, w_up, w_down, w_head),
+        (m_embed, m_bins, m_gains, m_qkv, m_out, m_up, m_down, m_head),
+        (v_embed, v_bins, v_gains, v_qkv, v_out, v_up, v_down, v_head),
+    )
+    return (*results[:24], stats[1, 0], query_count, results[24][0, 0])
 
 
 def solution(mesh):

time: 667 us -> 491 us (0.74)
  waiting for transfers between devices: 293 us -> 91.2 us
  Pallas kernels: 0 us -> 125 us
  blocking collectives: 116 us -> 47.6 us
  other arithmetic: 54.2 us -> 18.7 us
  local copies, waits for them, and re-layouts: 17.8 us -> 39.4 us
  starting transfers between devices: 9.84 us -> 0.34 us
  between operations: 24.6 us -> 17.8 us
    psum x3 -> x0, waiting for transfers between devices: 203 us -> none  [the longest x1 140 us: shards(): lax.psum(tuple((part.astype(HALF) for part in (grad_qkv, grad_out, grad_u...]
    pallas_call x0 -> x2, Pallas kernels: none -> 125 us  [the longest x1 101 us: reduce_gradients(): pl.pallas_call(kernel, out_shape=(jax.ShapeDtypeStruct((main_rows, width)...]
    psum x3 -> x0, blocking collectives: 69.4 us -> none  [the longest x1 39.8 us: shards(): lax.psum((grad_embed, grad_bins, gain_qry + gain_ctx), ('tables', 'heads'))]
    sub x8 -> x0, other arithmetic: 19.6 us -> none  [adam_update(): weight - rate * (first_hat / (jnp.sqrt(second_hat) + ADAM_EPS) + decay_ra...]
    unnamed x156 -> x176, local copies, waits for them, and re-layouts: 16.5 us -> 33.3 us
    reduce_sum x7 -> x0, other arithmetic: 12.4 us -> none  [the longest x1 2.84 us: shards(): jnp.sum(grad_up * grad_up)]
    psum x1, waiting for transfers between devices: 17.2 us -> 27.1 us  [shards(): back_norm_two = lax.psum(back_norm_two.astype(HALF), 'heads').astype(FLOAT)]
    psum x3 -> x0, starting transfers between devices: 9.42 us -> none  [the longest x1 9.34 us: shards(): lax.psum((grad_embed, grad_bins, gain_qry + gain_ctx), ('tables', 'heads'))]
  transfers between devices with their start and end apart: 7 -> 4, of which waited for: 6 -> 4; matrix products, arithmetic and copies ran while one was open for 18% -> 3% of each run, Pallas kernels for 0% -> 0%
where the time goes in v2:
time: 491 us; the launch traced here: 486 us
  matrix products  146 us (30%)
  Pallas kernels  125 us (25%)
  waiting for transfers between devices  91.2 us (19%)
  blocking collectives  47.6 us (10%)
  local copies, waits for them, and re-layouts  39.4 us (8%)
  other arithmetic  18.7 us (4%)
  between operations  17.8 us (4%)
    pallas_call x1, Pallas kernels, reduce_gradients(): pl.pallas_call(kernel, out_shape=(jax.ShapeDtypeStruct((main_rows, width)...  101 us
    all_gather x2, waiting for transfers between devices, gather(): return lax.all_gather(rows, 'heads', axis=axis, tiled=True)  36.9 us
    unnamed x176, local copies, waits for them, and re-layouts  33.3 us
    dot_general x1, matrix products, shards(): jnp.einsum('hbk,bhe->khe', back_scores, queries, preferred_element_type=F...  31.5 us
    dot_general x1, matrix products, shards(): jnp.einsum('hbk,khe->bhe', back_scores, key_heads, preferred_element_type...  29.3 us
    psum x1, waiting for transfers between devices, shards(): mlp = lax.psum(product(active, down_half).astype(HALF), 'heads')  27.1 us
    psum x1, waiting for transfers between devices, shards(): back_norm_two = lax.psum(back_norm_two.astype(HALF), 'heads').astype(FLOAT)  27.1 us
    pallas_call x1, Pallas kernels, adam_all(): pl.pallas_call(lambda *refs: adam_kernel(refs), grid=(steps,), in_specs=[...  24.2 us
  transfers between devices with their start and end apart: 4, of which 4 were waited for; matrix products, arithmetic and copies ran while one was open for 3% of the time, Pallas kernels for 0%

profile of v2, /device:TPU:0, one launch (start us, length us, event | category | flops | bytes accessed | tf_op | source)
XLA Modules:
  0.0 486.0 jit_solution(16465849199500487525)
XLA Ops:
  7.3 8.3 %all-gather.1 = bf16[1,2048,100]{1,2,0:T(8,128)(2,1)S(1)} all-gather(bf16[1,512,100]{1,2,0:T(8,128)(2,1)} %param.30), channel_id=3, replica_groups=mesh['tables'=8,'heads'=4] {'heads'}, dimensions={1}, use_global_device_ids=true | all-gather | bytes 512000 | tf_op jit(solution)/shard_map/all_gather | solution.py:62
  15.6 1.2 dynamic-slice
  17.5 0.9 add_dynamic-update-slice_fusion
  18.4 11.0 %all-reduce.2 = s32[3456]{0:T(1024)S(1)} all-reduce(s32[3456]{0:T(1024)S(1)} %add_dynamic-update-slice_fusion), channel_id=4, replica_groups=mesh['tables'=8,'heads'=4] {'heads'}, use_global_device_ids=true, to_apply=%add.2 | all-reduce | flops 3456 | bytes 27648
  29.5 1.4 slice_reduce_fusion
  31.0 2.0 fusion.82
  33.1 1.1 fusion.130
  35.0 2.1 copy-done.31
  37.2 0.8 multiply_convert_fusion.1
  38.0 0.8 convolution_convert_fusion.1
  38.8 1.7 convolution_convert_fusion
  40.6 6.1 %all-gather = bf16[1,704,100]{2,1,0:T(8,128)(2,1)S(1)} all-gather(bf16[1,176,100]{2,1,0:T(8,128)(2,1)S(1)} %copy-done.69), channel_id=2, replica_groups=mesh['tables'=8,'heads'=4] {'heads'}, dimensions={1}, use_global_device_ids=true | all-gather | bytes 176000 | tf_op jit(solution)/shard_map/all_gather | solution.py:62
  50.2 12.9 %fusion.132 = (f32[3,704]{1,0:T(4,128)}, f32[3,704,2048]{2,1,0:T(8,128)}) fusion(pred[2048]{0:T(1024)(128)(4,1)S(1)} %iota_compare_fusion.6, bf16[704,3,64]{0,2,1:T(8,128)(2,1)S(1)} %bitcast.108, bf16[2048,3,64]{0,2,1:T(8,128)(2,1)} %bitcast.101), kind=kOutput, calls=%fused_computation.201 | convolution fusion | flops 570951680 | bytes 18368768 | tf_op jit(solution)/shard_map/sub | solution.py:57
  63.1 9.4 %fusion.48 = bf16[3,64,704]{2,1,0:T(8,128)(2,1)} fusion(bf16[2048,3,64]{0,2,1:T(8,128)(2,1)S(1)} %bitcast.91, f32[3,704,2048]{2,1,0:T(8,128)} %get-tuple-element.171, f32[3,704]{1,0:T(4,128)} %get-tuple-element.170), kind=kOutput, calls=%fused_computation.73 | convolution fusion | flops 562434048 | bytes 18366720 | tf_op jit(solution)/shard_map/hbk,khe->bhe/dot_general | solution.py:455
  72.6 0.7 convert_element_type.170
  73.6 17.2 %all-gather.6.cloned.1.call-done = bf16[704,768]{0,1:T(8,128)(2,1)} async-done(((bf16[704,192]{0,1:T(8,128)(2,1)}), bf16[704,768]{0,1:T(8,128)(2,1)}) %all-gather.6.cloned.1.call-update) | async-done | bytes 1081360 | tf_op jit(solution)/shard_map/all_gather | solution.py:62
  90.8 19.6 %all-gather.8.cloned.1.call-done = bf16[768,768]{1,0:T(8,128)(2,1)} async-done(((bf16[192,768]{1,0:T(8,128)(2,1)}), bf16[768,768]{1,0:T(8,128)(2,1)}) %all-gather.8.cloned.1.call-update) | async-done | bytes 1179664 | tf_op jit(solution)/shard_map/all_gather | solution.py:62
  110.5 3.0 fusion.133
  113.9 1.1 fusion.74
  115.0 1.3 copy-done.47
  116.4 2.4 convolution_convert_fusion.5
  118.9 1.9 copy.69.refs_9_
  121.2 3.0 copy.71.refs_17_
  124.4 3.0 copy.73.refs_25_
  128.2 27.1 %all-reduce.6.cloned.1.call-done = bf16[704,768]{1,0:T(8,128)(2,1)} async-done(((bf16[704,768]{1,0:T(8,128)(2,1)}), bf16[704,768]{1,0:T(8,128)(2,1)}) %all-reduce.6.cloned.1.call-update) | async-done | bytes 1081360 | tf_op jit(solution)/shard_map/psum | solution.py:463
  155.3 2.2 fusion.128
  160.8 22.2 %psum.22 = f32[]{:T(128)} all-reduce(f32[]{:T(128)} %get-tuple-element.148), channel_id=1, replica_groups=mesh['tables'=8,'heads'=4] {'tables'}, use_global_device_ids=true, to_apply=%region_14.15 | all-reduce | flops 1 | bytes 8 | tf_op jit(solution)/shard_map/psum | solution.py:436
  183.7 2.7 multiply_reduce_fusion.4
  186.4 0.8 fusion.127
  187.3 0.8 copy-done.46
  188.1 1.4 copy-done.48
  189.5 2.3 fusion.45
  191.8 1.4 convolution_convert_fusion.2.refs_1_
  193.5 2.1 convolution_convert_fusion.4
  195.5 2.2 fusion.60
  199.0 4.9 %convolution_convert_fusion.3.refs_0_ = bf16[768,768]{1,0:T(8,128)(2,1)} fusion(f32[704,768]{1,0:T(8,128)} %copy-done.29, f32[704]{0:T(1024)S(1)} %negate_multiply_fusion.3, f32[704,768]{1,0:T(8,128)} %copy-done.47), kind=kOutput, calls=%fused_computation.70 | convolution fusion | flops 837009408 | bytes 5507840 | tf_op jit(solution)/shard_map/rf,rd->fd/dot_general | solution.py:477
  203.9 27.1 %all-reduce.8.cloned.1.call-done = bf16[704,768]{1,0:T(8,128)(2,1)} async-done(((bf16[704,768]{1,0:T(8,128)(2,1)}), bf16[704,768]{1,0:T(8,128)(2,1)}) %all-reduce.8.cloned.1.call-update) | async-done | bytes 1081360 | tf_op jit(solution)/shard_map/psum | solution.py:483
  231.0 2.6 fusion.37
  233.9 1.7 fusion.38
  235.6 1.2 add_add_fusion.4
  238.5 8.6 %fusion.29 = bf16[3,64,2048]{2,1,0:T(8,128)(2,1)} fusion(bf16[704,3,64]{0,2,1:T(8,128)(2,1)S(1)} %bitcast.99, f32[3,704,2048]{2,1,0:T(8,128)} %get-tuple-element.171, f32[3,704]{1,0:T(4,128)S(1)} %copy-done.77), kind=kOutput, calls=%fused_computation.39 | convolution fusion | flops 562692096 | bytes 18366720 | tf_op jit(solution)/shard_map/hbk,bhe->khe/dot_general | solution.py:490
  247.1 8.3 %fusion.135 = f32[3,704,2048]{2,1,0:T(8,128)} fusion(bf16[704,3,64]{0,2,1:T(8,128)(2,1)S(1)} %bitcast.100, bf16[2048,3,64]{0,2,1:T(8,128)(2,1)S(1)} %bitcast.92), kind=kOutput, calls=%fused_computation.204 | convolution fusion | flops 553648128 | bytes 18358272 | tf_op jit(solution)/shard_map/bhe,khe->hbk/dot_general | solution.py:493
  255.5 31.5 %fusion.32 = bf16[3,64,2048]{2,1,0:T(8,128)(2,1)} fusion(bf16[704,3,64]{0,2,1:T(8,128)(2,1)S(1)} %bitcast.109, f32[3,704,2048]{2,1,0:T(8,128)} %fusion.135, f32[3,704,2048]{2,1,0:T(8,128)} %get-tuple-element.171, f32[3,704]{1,0:T(4,128)} %get-tuple-element.170), kind=kOutput, calls=%fused_computation.40 | convolution fusion | flops 597299264 | bytes 35668224 | tf_op jit(solution)/shard_map/hbk,bhe->khe/dot_general | solution.py:499
  287.0 29.3 %fusion.51 = bf16[3,64,704]{2,1,0:T(8,128)(2,1)S(1)} fusion(bf16[2048,3,64]{0,2,1:T(8,128)(2,1)} %bitcast.102, f32[3,704,2048]{2,1,0:T(8,128)} %fusion.135, f32[3,704,2048]{2,1,0:T(8,128)} %get-tuple-element.171, f32[3,704]{1,0:T(4,128)} %get-tuple-element.170), kind=kOutput, calls=%fused_computation.76 | convolution fusion | flops 597041216 | bytes 35668224 | tf_op jit(solution)/shard_map/hbk,khe->bhe/dot_general | solution.py:498
  316.3 3.4 convolution_convert_fusion.7
  319.8 1.0 fusion.87
  321.7 0.9 multiply_reduce_fusion.5
  322.7 1.0 copy-done.16
  323.8 1.2 convolution_convert_fusion.6
  325.1 5.3 %multiply_reduce_fusion.1 = (f32[768]{0:T(1024)S(1)}, f32[2048]{0:T(1024)S(1)}, f32[2048,768]{0,1:T(8,128)S(1)}) fusion(f32[2048,768]{0,1:T(8,128)} %copy-done.14, f32[2048]{0:T(1024)S(1)} %copy-done.56, f32[2048]{0:T(1024)S(1)} %broadcast_multiply_fusion, f32[768]{0:T(1024)S(1)} %get-tuple-element.151, f32[2048,768]{0,1:T(8,128)S(1)} %fusion.87, ...), kind=kOutput, calls=%fused_computation.17 | convolution fusion | flops 616559872 | bytes 19987456 | tf_op jit(solution)/shard_map/rc,dc->rd/dot_general | solution.py:513
  330.5 2.6 fusion.126
  333.1 1.1 fusion.56
  334.2 1.6 fusion.61
  335.9 0.8 fusion.125
  338.8 101.1 %reduce_gradients.1 = (bf16[2304,768]{1,0:T(8,128)(2,1)S(1)}, bf16[256,768]{1,0:T(8,128)(2,1)S(1)}, f32[8,128]{1,0:T(8,128)S(1)}) custom-call(bf16[768,768]{1,0:T(8,128)(2,1)S(1)} %copy-done.3, bf16[768,768]{1,0:T(8,128)(2,1)S(1)} %convolution_convert_fusion.2.refs_1_, bf16[192,768]{1,0:T(8,128)(2,1)S(1)} %convolution_convert_fusion.10.refs_2_, ...), custom_call_target="tpu_custom_call" | custom-call | tf_op jit(solution)/shard_map/reduce_gradients/pallas_call | solution.py:275
  439.9 1.6 fusion.129
  441.6 1.0 slice.65.refs_4_
  443.3 24.2 %adam.1 = (f32[100,768]{1,0:T(8,128)}, f32[64,768]{1,0:T(8,128)}, f32[3,768]{1,0:T(4,128)}, f32[3,768,192]{2,1,0:T(8,128)}, f32[192,768]{1,0:T(8,128)}, /*index=...) custom-call(f32[8,128]{1,0:T(8,128)S(1)} %get-tuple-element.55.refs_, ...), custom_call_target="tpu_custom_call" | custom-call | tf_op jit(solution)/shard_map/adam/pallas_call | solution.py:371
  467.6 2.9 copy.75
  470.5 0.8 copy.76
  471.3 2.9 copy.77
  474.2 0.8 copy.78
  475.0 2.9 copy.79
  477.9 0.8 copy.80
  (226 shorter events, 16.5 us)
Async XLA Ops:
  7.2 83.6 %all-gather.6.cloned.1.call-start = ((), (), s32[]{:S(2)}) async-start(), calls=%async_computation | async-start | bytes 1474560 | tf_op jit(solution)/shard_map/all_gather | solution.py:62
  15.6 17.4 %copy-start.35 = (bf16[1,2048,100]{1,2,0:T(8,128)(2,1)}, bf16[1,2048,100]{1,2,0:T(8,128)(2,1)S(1)}, u32[]{:S(2)}) copy-start(bf16[1,2048,100]{1,2,0:T(8,128)(2,1)S(1)} %all-gather.1) | copy-start | bytes 1228804
  29.5 3.5 copy-start.60
  29.5 3.5 copy-start.62
  31.0 2.1 copy-start.4
  34.2 3.0 copy-start.14
  34.2 2.8 copy-start.31
  34.9 2.2 copy-start.64
  37.2 12.0 %copy-start.33 = (bf16[3,768,192]{1,2,0:T(8,128)(2,1)}, bf16[3,768,192]{1,2,0:T(8,128)(2,1)S(1)}, u32[]{:S(2)}) copy-start(bf16[3,768,192]{1,2,0:T(8,128)(2,1)S(1)} %convert_element_type.161) | copy-start | bytes 2654212
  38.0 2.6 copy-start.15
  38.8 24.3 %copy-start.41 = (bf16[2048,192]{0,1:T(8,128)(2,1)}, bf16[2048,192]{0,1:T(8,128)(2,1)S(1)}, u32[]{:S(2)}) copy-start(bf16[2048,192]{0,1:T(8,128)(2,1)S(1)} %convolution_convert_fusion.1) | copy-start | bytes 2359300
  38.8 1.8 copy-start.69
  38.8 7.8 %copy-start = (f32[100,768]{1,0:T(8,128)S(1)}, f32[100,768]{1,0:T(8,128)}, u32[]{:S(2)}) copy-start(f32[100,768]{1,0:T(8,128)} %refs_6_.1) | copy-start | bytes 921604
  46.6 1.6 copy-start.50
  47.2 63.3 %copy-start.20 = (f32[704,768]{1,0:T(8,128)}, f32[704,768]{1,0:T(8,128)S(1)}, u32[]{:S(2)}) copy-start(f32[704,768]{1,0:T(8,128)S(1)} %get-tuple-element.169) | copy-start | bytes 6488068
  50.2 12.9 %copy-start.75 = (bf16[704,192]{0,1:T(8,128)(2,1)}, bf16[704,192]{0,1:T(8,128)(2,1)S(1)}, u32[]{:S(2)}) copy-start(bf16[704,192]{0,1:T(8,128)(2,1)S(1)} %convolution_convert_fusion.11) | copy-start | bytes 811012
  63.1 9.5 %copy-start.2 = (f32[192,768]{1,0:T(8,128)S(1)}, f32[192,768]{1,0:T(8,128)}, u32[]{:S(2)}) copy-start(f32[192,768]{1,0:T(8,128)} %refs_10_.1) | copy-start | bytes 1769476
  72.5 37.9 %all-gather.8.cloned.1.call-start = ((), (), s32[]{:S(2)}) async-start(), calls=%async_computation.1 | async-start | bytes 1474560 | tf_op jit(solution)/shard_map/all_gather | solution.py:62
  73.4 82.0 %all-reduce.6.cloned.1.call-start = ((), (), s32[]{:S(2)}) async-start(), calls=%async_computation.2 | async-start | bytes 2162688 | tf_op jit(solution)/shard_map/psum | solution.py:463
  110.5 3.4 copy-start.27
  113.9 2.5 copy-start.45
  116.3 2.5 copy-start.32
  118.8 2.0 copy-start.61
  118.8 2.2 copy-start.49
  118.8 112.2 %all-reduce.8.cloned.1.call-start = ((), (), s32[]{:S(2)}) async-start(), calls=%async_computation.3 | async-start | bytes 2162688 | tf_op jit(solution)/shard_map/psum | solution.py:483
  121.2 3.0 copy-start.53
  124.4 3.0 copy-start.54
  183.7 2.7 copy-start.23
  186.4 1.7 copy-start.46
  186.4 3.1 copy-start.48
  187.3 4.5 copy-start.29
  189.5 2.3 copy-start.18
  191.8 1.7 copy-start.28
  231.0 2.6 copy-start.19
  231.0 2.9 copy-start.26
  233.6 2.0 copy-start.30
  236.8 1.7 copy-start.24
  236.8 1.7 copy-start.77
  238.5 8.6 %copy-start.42 = (bf16[2048,192]{0,1:T(8,128)(2,1)S(1)}, bf16[2048,192]{0,1:T(8,128)(2,1)}, u32[]{:S(2)}) copy-start(bf16[2048,192]{0,1:T(8,128)(2,1)} %copy-done.41) | copy-start | bytes 2359300
  247.1 8.4 %copy-start.76 = (bf16[704,192]{0,1:T(8,128)(2,1)S(1)}, bf16[704,192]{0,1:T(8,128)(2,1)}, u32[]{:S(2)}) copy-start(bf16[704,192]{0,1:T(8,128)(2,1)} %copy-done.75) | copy-start | bytes 811012
  316.3 3.5 copy-start.34
  316.3 3.5 copy-start.37
  319.8 1.9 copy-start.21
  319.8 1.9 copy-start.58
  319.8 1.9 copy-start.68
  321.7 1.9 copy-start.16
  321.7 2.1 copy-start.43
  322.6 2.4 copy-start.56
  323.8 6.6 %slice-start = ((s8[6291456]{0:T(1024)(128)(4,1)}), s8[4194304]{0:T(1024)(128)(4,1)S(1)}, s32[]{:S(2)}) async-start(s8[6291456]{0:T(1024)(128)(4,1)} %bitcast.87), calls=%async_computation.4 | async-start | bytes 8388608
  325.1 5.3 %copy-start.65 = (f32[2048]{0:T(1024)S(1)}, f32[2048]{0:T(1024)}, u32[]{:S(2)}) copy-start(f32[2048]{0:T(1024)} %copy-done.64) | copy-start | bytes 24580
  325.1 5.4 %slice-start.1 = ((s8[6291456]{0:T(1024)(128)(4,1)}), s8[2097152]{0:T(1024)(128)(4,1)S(1)}, s32[]{:S(2)}) async-start(s8[6291456]{0:T(1024)(128)(4,1)} %bitcast.87), calls=%async_computation.5 | async-start | bytes 4194304
  330.5 2.6 copy-start.36
  335.9 1.6 copy-start.25
  335.9 1.6 copy-start.51
  335.9 1.6 copy-start.74
  441.5 1.6 copy-start.5
  441.5 1.6 copy-start.6
  441.5 1.7 copy-start.7
  441.5 1.7 copy-start.8
  441.5 1.8 copy-start.9
  441.5 1.8 copy-start.10
  441.5 1.8 copy-start.11
  441.5 1.8 copy-start.12
  441.5 1.8 copy-start.13
  (20 other events, 22.8 us)
Sparse Core Ops, SparseCore 0:
  72.7 18.1 all-gather.5
  93.0 17.4 all-gather.7
  118.9 36.3 all-reduce.5
  197.9 33.0 all-reduce.7

commit v3 on v2

v3 whole, which is shorter than its diff:
```python
import jax
import jax.numpy as jnp
from jax import lax
from jax.experimental import pallas as pl
from jax.experimental.pallas import tpu as pltpu
from jax.sharding import PartitionSpec as P

HD = 64
BINS = 64
STEP = 10


NORM_EPS = 1e-05
ADAM_EPS = 1e-08
RATE = 0.05
RATE_WIDE = 1.0
BETA_ONE = 0.9
BETA_TWO = 0.95
DECAY = 0.1
CLIP_NORM = 0.02
MASKED = -1e30
FLOAT = jnp.float32
HALF = jnp.bfloat16
MESH = pl.DeviceIdType.MESH


def adam_update(weight, moment_one, moment_two, gradient, rate, decay_rate):
    moment_one = BETA_ONE * moment_one + (1.0 - BETA_ONE) * gradient
    moment_two = BETA_TWO * moment_two + (1.0 - BETA_TWO) * gradient * gradient
    first_hat = moment_one / (1.0 - BETA_ONE**STEP)
    second_hat = moment_two / (1.0 - BETA_TWO**STEP)
    weight = weight - rate * (first_hat / (jnp.sqrt(second_hat) + ADAM_EPS) + decay_rate * weight)
    return (weight, moment_one, moment_two)


def place_bit(place, bit):
    return lax.rem(lax.div(place, bit), 2)


def flip(place, bit):
    return place + bit - 2 * bit * place_bit(place, bit)


def bits_of(size):
    return [1 << power for power in range(size.bit_length() - 1)]


def partner(places, axis, bit):
    other = dict(places)
    other[axis] = flip(places[axis], bit)
    return (other["tables"], other["heads"])


def greet(places, axes):
    barrier = pltpu.get_barrier_semaphore()
    for axis, bit in axes:
        pl.semaphore_signal(
            barrier, inc=1, device_id=partner(places, axis, bit), device_id_type=MESH
        )
    pl.semaphore_wait(barrier, len(axes))


class Copies:
    def __init__(self, sends, recvs):
        self.sends, self.recvs, self.used = sends, recvs, 0

    def start(self, source, target, device):
        self.used += 1
        copy = pltpu.make_async_remote_copy(
            src_ref=source,
            dst_ref=target,
            send_sem=self.sends.at[self.used - 1],
            recv_sem=self.recvs.at[self.used - 1],
            device_id=device,
            device_id_type=MESH,
        )
        copy.start()
        return copy


class Landing:
    def __init__(self, rows_ref):
        self.rows_ref, self.used = rows_ref, 0

    def take(self, rows):
        self.used += rows
        return self.rows_ref.at[pl.ds(self.used - rows, rows), :]


def stages_of(rows, axes, least):
    steps = []
    for axis, bit in axes:
        if rows // 2 >= least and rows % 32 == 0:
            rows //= 2
            steps.append((axis, bit, "halve", rows))
        else:
            steps.append((axis, bit, "whole", rows))
    back = [(axis, bit, "back", left) for axis, bit, kind, left in reversed(steps) if kind == "halve"]
    return steps + back


def landing_rows(steps):
    return sum(left for _, _, kind, left in steps if kind != "back")


class Sum:
    def __init__(self, copies, landing, buffer, result, start, steps, places):
        self.copies, self.landing, self.buffer, self.result = copies, landing, buffer, result
        self.low, self.steps, self.places = start, steps, places
        self.at, self.copy, self.landed = 0, None, None

    def rows(self, low, count):
        if isinstance(low, int):
            return pl.ds(low, count)
        return pl.ds(pl.multiple_of(low, 16), count)

    def finish(self):
        if self.copy is None:
            return
        _, _, kind, count = self.steps[self.at - 1]
        self.copy.wait()
        self.copy = None
        if kind != "back":
            mine = self.rows(self.low, count)
            total = self.buffer[mine, :].astype(FLOAT) + self.landed[...].astype(FLOAT)
            last = self.at == len(self.steps) or self.steps[self.at][2] == "back"
            target = self.result if last else self.buffer
            target[mine, :] = total.astype(self.buffer.dtype)

    def start(self):
        if self.at >= len(self.steps):
            return
        axis, bit, kind, count = self.steps[self.at]
        self.at += 1
        side = place_bit(self.places[axis], bit)
        if kind == "halve":
            source = self.buffer.at[self.rows(self.low + count * (1 - side), count), :]
            self.low = self.low + count * side
            target = self.landed = self.landing.take(count)
        elif kind == "whole":
            source = self.buffer.at[self.rows(self.low, count), :]
            target = self.landed = self.landing.take(count)
        else:
            source = target = self.result.at[self.rows(self.low, count), :]
            self.low = self.low - count * side
        self.copy = self.copies.start(source, target, partner(self.places, axis, bit))

    def advance(self):
        self.finish()
        self.start()

    def done(self):
        return self.at >= len(self.steps) and self.copy is None


class Gather:
    def __init__(self, copies, views, places, bits):
        self.copies, self.views, self.places = copies, views, places
        self.bits, self.at, self.held, self.sent = bits, 0, [places["heads"]], []

    def finish(self):
        for copy in self.sent:
            copy.wait()
        if self.sent:
            self.held = self.held + [flip(slot, self.bits[self.at - 1]) for slot in self.held]
        self.sent = []

    def start(self):
        if self.at < len(self.bits):
            other = partner(self.places, "heads", self.bits[self.at])
            self.sent = [
                self.copies.start(view(slot), view(slot), other)
                for slot in self.held
                for view in self.views
            ]
            self.at += 1

    def advance(self):
        self.finish()
        self.start()

    def done(self):
        return self.at >= len(self.bits) and not self.sent


def places_here():
    return {"tables": lax.axis_index("tables"), "heads": lax.axis_index("heads")}


SMALL = {"head": (0, 64), "bins": (64, 64), "embed": (128, 112), "gains": (240, 16)}
SMALL_ROWS = 256
CHUNK = 256


def dot(left, right, over=(1, 0)):
    return lax.dot_general(
        left, right, (((over[0],), (over[1],)), ((), ())), preferred_element_type=FLOAT
    )


def standard(rows):
    center = rows - jnp.mean(rows, axis=-1, keepdims=True)
    scale = lax.rsqrt(jnp.mean(center * center, axis=-1, keepdims=True) + NORM_EPS)
    return center * scale, scale


def standard_back(upstream, gain_row, unit, scale):
    inner = upstream * gain_row
    lean = jnp.mean(inner, axis=-1, keepdims=True)
    tilt = jnp.mean(inner * unit, axis=-1, keepdims=True)
    return (inner - lean - unit * tilt) * scale


def as_row(column):
    return jnp.broadcast_to(column, (column.shape[0], 128)).T[:1]


def as_column(row):
    return jnp.broadcast_to(row, (8, row.shape[1])).T[:, :1]


def column_sums(rows):
    return jnp.sum(rows, axis=0, keepdims=True)


def gelu_both(hidden):
    root = 0.7978845608028654
    square = hidden * hidden
    bent = jnp.tanh(root * hidden * (1.0 + 0.044715 * square))
    half = 0.5 * (1.0 + bent)
    slope = half + 0.5 * hidden * (1.0 - bent * bent) * root * (1.0 + 0.134145 * square)
    return hidden * half, slope


def sum_squares(rows_ref, count):
    def piece(step, total):
        part = rows_ref[pl.ds(pl.multiple_of(step * 64, 64), 64), :].astype(FLOAT)
        return total + jnp.sum((part * part).reshape(8, 8, part.shape[1]), axis=0)

    return lax.fori_loop(0, count // 64, piece, jnp.zeros((8, rows_ref.shape[1]), FLOAT))


def one_value(total):
    return jnp.sum(jnp.sum(total, axis=0, keepdims=True), axis=1, keepdims=True)


class Named:
    pass


def train_kernel(shape, r):
    groups, ctx, qry, width, inner, hidden = (
        shape.groups,
        shape.ctx,
        shape.qry,
        shape.width,
        shape.inner,
        shape.hidden,
    )
    heads = inner // HD
    total_ctx, total_qry = groups * ctx, groups * qry
    block = 2 * qry
    blocks = total_qry // block
    half = width // 2
    places = places_here()
    me = places["heads"]
    copies = Copies(r.sends, r.recvs)
    over_heads, over_tables = shape.over_heads, shape.over_tables
    far_first = [bit for _, bit in reversed(over_heads)]
    tiny = Landing(r.tiny_land)
    wide = Landing(r.wide_land)
    narrow = Landing(r.narrow_land)
    greet(places, over_heads + over_tables)

    r.feat[me, pl.ds(0, ctx), :] = r.ctx_feat[...]
    r.feat[me, pl.ds(ctx, qry), :] = r.qry_feat[...]
    r.ints[me] = jnp.zeros((8, ctx), jnp.int32)
    r.ints[me, 0:1, :] = r.ctx_bins[...]
    r.ints[me, 1:2, pl.ds(0, qry)] = r.qry_bins[...]
    r.ints[me, 2:3, pl.ds(0, qry)] = r.query_mask[...]
    rows_in = Gather(
        copies,
        [lambda slot: r.feat.at[slot], lambda slot: r.ints.at[slot]],
        places,
        far_first,
    )
    rows_in.start()
    mask_sum = jnp.sum(r.query_mask[...].astype(FLOAT), axis=1, keepdims=True)
    r.count_work[...] = jnp.broadcast_to(mask_sum, (16, 128))
    tiny_steps = stages_of(16, over_heads + over_tables, 16)
    counted = Sum(copies, tiny, r.count_work, r.count, 0, tiny_steps, places)
    counted.start()
    r.out_all[me] = r.w_out[...]
    outs_in = Gather(copies, [lambda slot: r.out_all.at[slot]], places, far_first)

    embed_half = r.w_embed[...].astype(HALF)
    bins_half = r.w_bins[...].astype(HALF)
    gain_one, gain_two, gain_last = (r.gains[row : row + 1, :] for row in range(3))
    bin_rows = lax.broadcasted_iota(jnp.int32, (BINS, 256), 0)

    def one_hot(slot, place):
        return jnp.where(
            bin_rows == r.ints[slot, 0:1, pl.ds(pl.multiple_of(place * 256, 256), 256)], 1.0, 0.0
        ).astype(HALF)

    def embed_shard(slot):
        def context(place, _):
            at = pl.multiple_of(slot * ctx + place * 256, 256)
            feat = r.feat[slot, pl.ds(pl.multiple_of(place * 256, 256), 256), :]
            zero = dot(feat, embed_half) + dot(one_hot(slot, place), bins_half, (0, 0))
            unit, scale = standard(zero)
            normed = (unit * gain_one).astype(HALF)
            r.normed_ctx[pl.ds(at, 256), :] = normed
            r.scale_ctx[pl.ds(slot * (ctx // 256) + place, 1), :] = as_row(scale)
            keys = dot(normed, r.w_qkv[1], (1, 1))
            values = dot(normed, r.w_qkv[2], (1, 1))
            r.keys[pl.ds(at, 256), :] = keys.astype(HALF)
            r.values[pl.ds(at, 256), :] = values.astype(HALF)
            r.keys_t[:, pl.ds(at, 256)] = keys.T.astype(HALF)
            r.values_t[:, pl.ds(at, 256)] = values.T.astype(HALF)
            return 0

        lax.fori_loop(0, ctx // 256, context, 0)
        at = pl.multiple_of(slot * qry, 16)
        zero = dot(r.feat[slot, pl.ds(ctx, qry), :], embed_half)
        r.stream[pl.ds(at, qry), :] = zero
        unit, scale = standard(zero)
        normed = (unit * gain_one).astype(HALF)
        r.normed_qry[pl.ds(at, qry), :] = normed
        r.scale_qry[pl.ds(slot, 1), :] = as_row(scale)
        queries = dot(normed, r.w_qkv[0], (1, 1))
        r.queries[pl.ds(at, qry), :] = queries.astype(HALF)
        r.queries_t[slot] = queries.T.astype(HALF)

    done = 0
    while done < groups:
        for slot in rows_in.held[done:]:
            embed_shard(slot)
            done += 1
            counted.advance()
            outs_in.advance()
        rows_in.advance()
    while not counted.done() and counted.at < len(counted.steps):
        counted.advance()

    lane = lax.broadcasted_iota(jnp.int32, (1, inner), 1)
    head_rows = [
        jnp.where((lane >= h * HD) & (lane < (h + 1) * HD), 1.0, 0.0).astype(FLOAT)
        for h in range(heads)
    ]
    slots_at = lax.broadcasted_iota(jnp.int32, (1, total_ctx), 1)
    dead = jnp.where(slots_at < r.counts[0], 0.0, MASKED)
    mixing = []
    for b in range(groups):
        rows = pl.ds(b * qry, qry)
        query_blk = r.queries[rows, :]
        mixed = jnp.zeros((qry, inner), FLOAT)
        for h in range(heads):
            raw = dot(query_blk * (head_rows[h] * HD**-0.5).astype(HALF), r.keys_t[...]) + dead
            raised = jnp.exp(raw - jnp.max(raw, axis=-1, keepdims=True))
            weights = (raised * (1.0 / jnp.sum(raised, axis=-1, keepdims=True))).astype(HALF)
            r.weights[h, rows, :] = weights
            mixed = mixed + dot(weights, r.values[...]) * head_rows[h]
        r.mixed[rows, :] = mixed
        r.mix_all[me, b] = mixed.astype(HALF)
        mixing.append(
            Gather(copies, [lambda slot, b=b: r.mix_all.at[slot, b]], places, far_first)
        )
        for gathering in mixing:
            gathering.advance()
        outs_in.advance()
    while not outs_in.done():
        outs_in.advance()
    while not counted.done():
        counted.advance()

    sum_steps = stages_of(2 * block, over_heads, block)
    down_sums, back_sums = [], []
    for b in range(blocks):
        for part in range(2 * b, 2 * b + 2):
            while not mixing[part].done():
                mixing[part].advance()
        rows = pl.ds(b * block, block)
        attended = []
        for part in range(2 * b, 2 * b + 2):
            total = dot(r.mix_all[0, part], r.out_all[0])
            for slot in range(1, groups):
                total = total + dot(r.mix_all[slot, part], r.out_all[slot])
            attended.append(total)
        stream = r.stream[rows, :] + jnp.concatenate(attended, axis=0)
        r.stream[rows, :] = stream
        unit, _ = standard(stream)
        normed = (unit * gain_two).astype(HALF)
        r.normed_two[rows, :] = normed
        active, slope = gelu_both(dot(normed, r.w_up[...]))
        active = active.astype(HALF)
        r.active[rows, :] = active
        r.slope[rows, :] = slope.astype(HALF)
        low = pl.ds(2 * b * block, block)
        high = pl.ds((2 * b + 1) * block, block)
        part = dot(active, r.w_down[...]).astype(HALF)
        r.down_work[low, :] = part[:, :half]
        r.down_work[high, :] = part[:, half:]
        summing = Sum(
            copies, narrow, r.down_work, r.down_sum, 2 * b * block, sum_steps, places
        )
        down_sums.append(summing)
        summing.start()
        for earlier in down_sums[:-1]:
            earlier.advance()

    head_half = r.w_head[...].astype(HALF)
    divisor = jnp.maximum(r.count[0:1, 0:1], 1.0)
    tall = lax.broadcasted_iota(jnp.int32, (BINS, 256), 0)
    loss = jnp.zeros((1, 1), FLOAT)
    grad_head = jnp.zeros((BINS, width), FLOAT)
    gain_sum_last = jnp.zeros((1, width), FLOAT)
    for b in range(blocks):
        for later in down_sums[b + 1 :]:
            later.advance()
        while not down_sums[b].done():
            down_sums[b].advance()
        rows = pl.ds(b * block, block)
        low = pl.ds(2 * b * block, block)
        high = pl.ds((2 * b + 1) * block, block)
        mlp = jnp.concatenate([r.down_sum[low, :], r.down_sum[high, :]], axis=1)
        unit, scale = standard(r.stream[rows, :] + mlp.astype(FLOAT))
        normed = (unit * gain_last).astype(HALF)
        logits = dot(normed, head_half, (1, 1))
        targets, masks = [], []
        for slot in range(2 * b, 2 * b + 2):
            target = jnp.where(tall == r.ints[slot, 1:2, 0:256], 1.0, 0.0)
            targets.append(target.T[:qry])
            mask = jnp.broadcast_to(r.ints[slot, 2:3, 0:256].astype(FLOAT), (8, 256))
            masks.append(mask.T[:qry, :1])
        target = jnp.concatenate(targets, axis=0)
        mask = jnp.concatenate(masks, axis=0)
        top = jnp.max(logits, axis=-1, keepdims=True)
        log_bins = top + jnp.log(jnp.sum(jnp.exp(logits - top), axis=-1, keepdims=True))
        missed = log_bins - jnp.sum(target * logits, axis=-1, keepdims=True)
        loss = loss + jnp.sum(mask * missed, axis=0, keepdims=True)
        back_logits = (mask * (jnp.exp(logits - log_bins) - target) / divisor).astype(HALF)
        grad_head = grad_head + dot(back_logits, normed, (0, 0))
        back_final = dot(back_logits, head_half)
        gain_sum_last = gain_sum_last + column_sums(back_final * unit)
        back_two = standard_back(back_final, gain_last, unit, scale)
        r.back[rows, :] = back_two
        back_mlp = back_two.astype(HALF)
        r.back_mlp[rows, :] = back_mlp
        back_active = dot(back_mlp, r.w_down[...], (1, 1))
        back_up = (r.slope[rows, :].astype(FLOAT) * back_active).astype(HALF)
        r.back_up[rows, :] = back_up
        part = dot(back_up, r.w_up[...], (1, 1)).astype(HALF)
        r.down_work[low, :] = part[:, :half]
        r.down_work[high, :] = part[:, half:]
        summing = Sum(
            copies, narrow, r.down_work, r.down_sum, 2 * b * block, sum_steps, places
        )
        back_sums.append(summing)
        summing.start()
        for earlier in back_sums[:-1]:
            earlier.advance()
    r.loss_work[...] = jnp.broadcast_to(loss / groups, (16, 128))
    losses = Sum(copies, tiny, r.loss_work, r.loss, 0, tiny_steps, places)
    losses.start()
    r.small[pl.ds(0, BINS), :] = grad_head / groups

    main_steps = stages_of(CHUNK, over_tables, 16)
    mains = []

    def pump():
        for part in mains:
            part.advance()
        losses.advance()

    def send_chunk(place):
        part = Sum(copies, wide, r.main_work, r.main, CHUNK * place, main_steps, places)
        part.start()
        mains.append(part)

    for place in range(hidden // CHUNK):
        at = pl.ds(place * CHUNK, CHUNK)
        r.main_work[at, :] = dot(r.active[:, at], r.back_mlp[...], (0, 0)).astype(HALF)
        send_chunk(len(mains))
        for summing in back_sums:
            summing.advance()
    for place in range(width // CHUNK):
        at = pl.ds(place * CHUNK, CHUNK)
        to = pl.ds(hidden + place * CHUNK, CHUNK)
        r.main_work[to, :] = dot(r.normed_two[:, at], r.back_up[...], (0, 0)).astype(HALF)
        send_chunk(len(mains))
        for summing in back_sums:
            summing.advance()

    gain_sum_two = jnp.zeros((1, width), FLOAT)
    r.keys_back[...] = jnp.zeros(r.keys_back.shape, FLOAT)
    r.values_back[...] = jnp.zeros(r.values_back.shape, FLOAT)
    for b in range(blocks):
        for later in back_sums[b + 1 :]:
            later.advance()
        while not back_sums[b].done():
            back_sums[b].advance()
        rows = pl.ds(b * block, block)
        low = pl.ds(2 * b * block, block)
        high = pl.ds((2 * b + 1) * block, block)
        upstream = jnp.concatenate([r.down_sum[low, :], r.down_sum[high, :]], axis=1).astype(FLOAT)
        unit, scale = standard(r.stream[rows, :])
        gain_sum_two = gain_sum_two + column_sums(upstream * unit)
        back_one = r.back[rows, :] + standard_back(upstream, gain_two, unit, scale)
        r.back[rows, :] = back_one
        back_attn = back_one.astype(HALF)
        r.slope[rows, :] = back_attn
        back_mix = dot(back_attn, r.w_out[...], (1, 1)).astype(HALF)
        r.back_mix[rows, :] = back_mix
        turned = back_mix.astype(FLOAT)
        for part in range(2):
            r.back_mix_t[2 * b + part] = turned[part * qry : (part + 1) * qry].T.astype(HALF)
        pump()
        for h in range(heads):

            def backward(part, _, h=h):
                here = 2 * b + part
                at = pl.ds(pl.multiple_of(here * qry, 16), qry)
                back_mix = r.back_mix[at, :]
                mine = back_mix * head_rows[h].astype(HALF)
                lean = jnp.sum(
                    mine.astype(FLOAT) * r.mixed[at, :], axis=-1, keepdims=True
                )
                weights = r.weights[h, at, :]
                back_weights = dot(mine, r.values_t[...])
                back_scores = (weights.astype(FLOAT) * (back_weights - lean)).astype(HALF)
                queries_back = dot(back_scores, r.keys[...]) * (head_rows[h] * HD**-0.5)
                if h == 0:
                    r.queries_back[at, :] = queries_back
                else:
                    r.queries_back[at, :] += queries_back
                lanes = pl.ds(h * HD, HD)
                r.values_back[lanes, :] += dot(r.back_mix_t[here, lanes, :], weights)
                r.keys_back[lanes, :] += dot(r.queries_t[here, lanes, :], back_scores)
                return 0

            lax.fori_loop(0, 2, backward, 0)
            pump()

    first = hidden + width
    pieces = [
        lambda: dot(r.mix_all[me].reshape(total_qry, inner), r.slope[...], (0, 0)),
        lambda: dot(r.queries_back[...].astype(HALF), r.normed_qry[...], (0, 0)),
        lambda: dot((r.keys_back[...] * HD**-0.5).astype(HALF), r.normed_ctx[...]),
        lambda: dot(r.values_back[...].astype(HALF), r.normed_ctx[...]),
    ]
    for place, piece in enumerate(pieces):
        r.main_work[pl.ds(first + place * inner, inner), :] = piece().astype(HALF)
        while (len(mains) + 1) * CHUNK <= first + (place + 1) * inner:
            send_chunk(len(mains))
        pump()

    over_gain = 1.0 / gain_one
    low_bins, low_embed, low_gains = (SMALL[name][0] for name in ("bins", "embed", "gains"))
    features = r.w_embed.shape[0]
    r.small[pl.ds(BINS, SMALL_ROWS - BINS), :] = jnp.zeros((SMALL_ROWS - BINS, width), FLOAT)
    bins_at = pl.ds(low_bins, BINS)
    embed_at = pl.ds(low_embed, features)

    def embed_back(upstream, normed, scale):
        unit = normed.astype(FLOAT) * over_gain
        return column_sums(upstream * unit), standard_back(upstream, gain_one, unit, scale)

    def context_back(place, gain_sum):
        slot, offset = lax.div(place, ctx // 256), lax.rem(place, ctx // 256)
        at = pl.ds(pl.multiple_of(place * 256, 256), 256)
        keys = (r.keys_back[:, at] * HD**-0.5).T.astype(HALF)
        values = r.values_back[:, at].T.astype(HALF)
        upstream = dot(keys, r.w_qkv[1]) + dot(values, r.w_qkv[2])
        gains, back_zero = embed_back(upstream, r.normed_ctx[at, :], as_column(r.scale_ctx[pl.ds(place, 1), :]))
        back_zero = back_zero.astype(HALF)
        feat = r.feat[slot, pl.ds(pl.multiple_of(offset * 256, 256), 256), :]
        r.small[embed_at, :] += dot(feat, back_zero, (0, 0))
        r.small[bins_at, :] += dot(one_hot(slot, offset), back_zero)
        return gain_sum + gains

    gain_sum_one = jnp.zeros((1, width), FLOAT)
    pieces = total_ctx // 256
    for part in range(2):
        gain_sum_one = lax.fori_loop(
            part * pieces // 2, (part + 1) * pieces // 2, context_back, gain_sum_one
        )
        pump()

    def query_back(slot, gain_sum):
        at = pl.ds(pl.multiple_of(slot * qry, 16), qry)
        upstream = dot(r.queries_back[at, :].astype(HALF), r.w_qkv[0])
        gains, back_zero = embed_back(upstream, r.normed_qry[at, :], as_column(r.scale_qry[pl.ds(slot, 1), :]))
        mine = jnp.where(slot == me, 1.0, 0.0)
        back_zero = (back_zero + mine * r.back[at, :]).astype(HALF)
        feat = r.feat[slot, pl.ds(ctx, qry), :]
        r.small[embed_at, :] += dot(feat, back_zero, (0, 0))
        return gain_sum + gains

    gain_sum_one = lax.fori_loop(0, groups, query_back, gain_sum_one)
    r.small[pl.ds(low_gains, 1), :] = gain_sum_one
    r.small[pl.ds(low_gains + 1, 1), :] = gain_sum_two / groups
    r.small[pl.ds(low_gains + 2, 1), :] = gain_sum_last / groups
    r.small_work[...] = r.small[...].astype(HALF)

    small_steps = stages_of(SMALL_ROWS, over_heads + over_tables, 64)
    smalls = Sum(copies, wide, r.small_work, r.small_out, 0, small_steps, places)
    smalls.start()
    waiting = len(over_heads)
    while not all(part.done() for part in mains) or smalls.at < len(small_steps) - waiting:
        pump()
        if smalls.at < len(small_steps) - waiting:
            smalls.advance()
    while not losses.done():
        losses.advance()
    squares = one_value(sum_squares(r.main, r.main.shape[0]))
    r.square_work[...] = jnp.broadcast_to(squares, (16, 128))
    square_steps = stages_of(16, list(reversed(over_heads)), 16)
    squared = Sum(copies, tiny, r.square_work, r.square, 0, square_steps, places)
    while not (squared.done() and smalls.done()):
        smalls.advance()
        squared.advance()
    squares = r.square[0:8, :] + one_value(sum_squares(r.small_out, SMALL_ROWS))
    row = lax.broadcasted_iota(jnp.int32, (8, 128), 0)
    r.stats[...] = jnp.where(row == 0, squares, jnp.where(row == 1, r.loss[0:8, :], r.count[0:8, :]))


def train(sizes, inputs):
    shape = Named()
    shape.groups = sizes["heads"]
    shape.ctx, features = inputs["ctx_feat"].shape
    shape.qry = inputs["qry_feat"].shape[0]
    shape.width = inputs["w_embed"].shape[1]
    shape.inner = inputs["w_out"].shape[0]
    shape.hidden = inputs["w_up"].shape[1]
    shape.over_tables = [("tables", bit) for bit in bits_of(sizes["tables"])]
    shape.over_heads = [("heads", bit) for bit in bits_of(sizes["heads"])]
    groups, ctx, qry, width, inner, hidden = (
        shape.groups,
        shape.ctx,
        shape.qry,
        shape.width,
        shape.inner,
        shape.hidden,
    )
    total_ctx, total_qry = groups * ctx, groups * qry
    heads = inner // HD
    main_rows = hidden + width + 4 * inner
    block = 2 * qry
    main_steps = stages_of(CHUNK, shape.over_tables, 16)
    small_steps = stages_of(SMALL_ROWS, shape.over_heads + shape.over_tables, 64)
    sum_steps = stages_of(2 * block, shape.over_heads, block)
    wide_rows = main_rows // CHUNK * landing_rows(main_steps) + landing_rows(small_steps)
    narrow_rows = 2 * (total_qry // block) * landing_rows(sum_steps)
    every = len(shape.over_tables) + len(shape.over_heads)
    tiny_rows = 16 * (2 * every + len(shape.over_heads))
    tiny = ((16, 128), FLOAT)
    scratch = {
        "feat": ((groups, ctx + qry, features), HALF),
        "ints": ((groups, 8, ctx), jnp.int32),
        "out_all": ((groups, inner, width), HALF),
        "count_work": tiny,
        "count": tiny,
        "loss_work": tiny,
        "loss": tiny,
        "square_work": tiny,
        "square": tiny,
        "normed_ctx": ((total_ctx, width), HALF),
        "scale_ctx": ((total_ctx // 256, 256), FLOAT),
        "normed_qry": ((total_qry, width), HALF),
        "scale_qry": ((groups, qry), FLOAT),
        "stream": ((total_qry, width), FLOAT),
        "queries": ((total_qry, inner), HALF),
        "queries_t": ((groups, inner, qry), HALF),
        "keys": ((total_ctx, inner), HALF),
        "values": ((total_ctx, inner), HALF),
        "keys_t": ((inner, total_ctx), HALF),
        "values_t": ((inner, total_ctx), HALF),
        "weights": ((heads, total_qry, total_ctx), HALF),
        "mixed": ((total_qry, inner), FLOAT),
        "mix_all": ((groups, groups, qry, inner), HALF),
        "normed_two": ((total_qry, width), HALF),
        "active": ((total_qry, hidden), HALF),
        "slope": ((total_qry, hidden), HALF),
        "down_work": ((2 * total_qry, width // 2), HALF),
        "down_sum": ((2 * total_qry, width // 2), HALF),
        "back": ((total_qry, width), FLOAT),
        "back_mlp": ((total_qry, width), HALF),
        "back_up": ((total_qry, hidden), HALF),
        "back_mix": ((total_qry, inner), HALF),
        "back_mix_t": ((groups, inner, qry), HALF),
        "queries_back": ((total_qry, inner), FLOAT),
        "keys_back": ((inner, total_ctx), FLOAT),
        "values_back": ((inner, total_ctx), FLOAT),
        "main_work": ((main_rows, width), HALF),
        "small": ((SMALL_ROWS, width), FLOAT),
        "small_work": ((SMALL_ROWS, width), HALF),
        "wide_land": ((wide_rows, width), HALF),
        "narrow_land": ((narrow_rows, width // 2), HALF),
        "tiny_land": ((tiny_rows, 128), FLOAT),
    }
    outputs = {
        "main": jax.ShapeDtypeStruct((main_rows, width), HALF),
        "small_out": jax.ShapeDtypeStruct((SMALL_ROWS, width), HALF),
        "stats": jax.ShapeDtypeStruct((8, 128), FLOAT),
    }
    names = list(inputs) + list(outputs) + list(scratch) + ["sends", "recvs"]

    def kernel(*refs):
        named = Named()
        named.__dict__.update(zip(names, refs))
        train_kernel(shape, named)

    whole = pl.BlockSpec(memory_space=pltpu.VMEM)
    semaphores = pltpu.SemaphoreType.DMA((160,))
    return pl.pallas_call(
        kernel,
        out_shape=tuple(outputs.values()),
        in_specs=[
            pl.BlockSpec(memory_space=pltpu.SMEM) if name == "counts" else whole for name in inputs
        ],
        out_specs=(whole,) * 3,
        scratch_shapes=[pltpu.VMEM(size, kind) for size, kind in scratch.values()]
        + [semaphores, semaphores],
        compiler_params=pltpu.CompilerParams(
            collective_id=1, has_side_effects=True, vmem_limit_bytes=60 * 2**20
        ),
        name="train",
    )(*inputs.values())


def adam_kernel(refs):
    (stats, main_d, main_u, main_o, main_q, main_k, main_v, small) = refs[:8]
    w = refs[8:16]
    m = refs[16:24]
    v = refs[24:32]
    w_new = refs[32:40]
    m_new = refs[40:48]
    v_new = refs[48:56]
    norm_ref = refs[56]
    norm = jnp.sqrt(stats[0:1, 0:1])
    norm_ref[...] = jnp.broadcast_to(norm, norm_ref.shape)
    factor = jnp.minimum(1.0, CLIP_NORM / (norm + 1e-06))

    def update(which, gradient, rate, decay, at=...):
        gradient = gradient.astype(FLOAT) * factor
        results = adam_update(w[which][at], m[which][at], v[which][at], gradient, rate, decay)
        for target, value in zip((w_new, m_new, v_new), results):
            target[which][at] = value

    update(6, main_d[...], RATE, DECAY)
    update(5, main_u[...], RATE, DECAY)
    update(4, main_o[...], RATE_WIDE, DECAY)
    for part, gradient in enumerate((main_q, main_k, main_v)):
        update(3, gradient[...], RATE, DECAY, at=part)

    @pl.when(pl.program_id(0) == 0)
    def _():
        def rows(name, count):
            low, size = SMALL[name]
            return small[low : low + size, :].astype(FLOAT)[:count]

        update(0, rows("embed", w[0].shape[0]), RATE, DECAY)
        update(1, rows("bins", w[1].shape[0]), RATE_WIDE, DECAY)
        update(2, rows("gains", w[2].shape[0]), RATE_WIDE, 0.0)
        update(7, rows("head", w[7].shape[0]), RATE, DECAY)


def adam_all(stats, main, small, weights, firsts, seconds):
    inner, width = weights[4].shape
    hidden = weights[5].shape[1]
    steps = 6

    def fixed(array):
        return pl.BlockSpec(array.shape, lambda step: (0,) * array.ndim)

    def rows_of(rows, low=0):
        size = rows // steps
        return pl.BlockSpec((size, width), lambda step: (low // size + step, 0))

    blocks = [
        fixed(weights[0]),
        fixed(weights[1]),
        fixed(weights[2]),
        pl.BlockSpec((3, inner // steps, width), lambda step: (0, step, 0)),
        rows_of(inner),
        pl.BlockSpec((width // steps, hidden), lambda step: (step, 0)),
        rows_of(hidden),
        fixed(weights[7]),
    ]
    first = hidden + width
    shapes = [jax.ShapeDtypeStruct(weight.shape, FLOAT) for weight in weights]
    return pl.pallas_call(
        lambda *refs: adam_kernel(refs),
        grid=(steps,),
        in_specs=[fixed(stats), rows_of(hidden), rows_of(width, hidden)]
        + [rows_of(inner, first + part * inner) for part in range(4)]
        + [fixed(small)]
        + blocks * 3,
        out_specs=blocks * 3 + [fixed(stats)],
        out_shape=shapes * 3 + [jax.ShapeDtypeStruct(stats.shape, FLOAT)],
        compiler_params=pltpu.CompilerParams(vmem_limit_bytes=48 * 2**20),
        name="adam",
    )(stats, *[main] * 6, small, *weights, *firsts, *seconds)


def shards(
    ctx_feat,
    qry_feat,
    counts,
    ctx_bins,
    qry_bins,
    query_mask,
    w_embed,
    w_bins,
    norm_gains,
    w_qkv,
    w_out,
    w_up,
    w_down,
    w_head,
    m_embed,
    m_bins,
    m_gains,
    m_qkv,
    m_out,
    m_up,
    m_down,
    m_head,
    v_embed,
    v_bins,
    v_gains,
    v_qkv,
    v_out,
    v_up,
    v_down,
    v_head,
):
    sizes = {"tables": lax.axis_size("tables"), "heads": lax.axis_size("heads")}
    main, small, stats = train(
        sizes,
        {
            "counts": counts,
            "ctx_feat": ctx_feat[0],
            "qry_feat": qry_feat[0],
            "ctx_bins": ctx_bins,
            "qry_bins": qry_bins,
            "query_mask": query_mask,
            "w_embed": w_embed,
            "w_bins": w_bins,
            "gains": norm_gains,
            "w_qkv": jnp.swapaxes(w_qkv, 1, 2).astype(HALF),
            "w_out": w_out.astype(HALF),
            "w_up": w_up.astype(HALF),
            "w_down": w_down.astype(HALF),
            "w_head": w_head.T,
        },
    )
    results = adam_all(
        stats,
        main,
        small,
        *(
            (embed, bins, gains, jnp.swapaxes(qkv, 1, 2), out, up, down, head.T)
            for embed, bins, gains, qkv, out, up, down, head in (
                (w_embed, w_bins, norm_gains, w_qkv, w_out, w_up, w_down, w_head),
                (m_embed, m_bins, m_gains, m_qkv, m_out, m_up, m_down, m_head),
                (v_embed, v_bins, v_gains, v_qkv, v_out, v_up, v_down, v_head),
            )
        ),
    )
    *updated, norm = results
    for low in range(0, 24, 8):
        updated[low + 3] = jnp.swapaxes(updated[low + 3], 1, 2)
        updated[low + 7] = updated[low + 7].T
    return (*updated, stats[1, 0], stats[2, 0], norm[0, 0])


def solution(mesh):
    in_specs = (
        P("tables", "heads", None),
        P("tables", "heads", None),
        P("tables"),
        P("tables", "heads"),
        P("tables", "heads"),
        P("tables", "heads"),
        P(),
        P(),
        P(),
        P(None, None, "heads"),
        P("heads", None),
        P(None, "heads"),
        P("heads", None),
        P(),
        P(),
        P(),
        P(),
        P(None, None, "heads"),
        P("heads", None),
        P(None, "heads"),
        P("heads", None),
        P(),
        P(),
        P(),
        P(),
        P(None, None, "heads"),
        P("heads", None),
        P(None, "heads"),
        P("heads", None),
        P(),
    )
    out_specs = (
        P(),
        P(),
        P(),
        P(None, None, "heads"),
        P("heads", None),
        P(None, "heads"),
        P("heads", None),
        P(),
        P(),
        P(),
        P(),
        P(None, None, "heads"),
        P("heads", None),
        P(None, "heads"),
        P("heads", None),
        P(),
        P(),
        P(),
        P(),
        P(None, None, "heads"),
        P("heads", None),
        P(None, "heads"),
        P("heads", None),
        P(),
        P(),
        P(),
        P(),
    )
    return jax.shard_map(shards, mesh=mesh, in_specs=in_specs, out_specs=out_specs, check_vma=False)
```

time: 491 us -> 263 us (0.54)
  matrix products: 146 us -> 0 us
  Pallas kernels: 125 us -> 242 us
  waiting for transfers between devices: 91.2 us -> 0 us
  blocking collectives: 47.6 us -> 0 us
  local copies, waits for them, and re-layouts: 39.4 us -> 9.21 us
  between operations: 17.8 us -> 1.97 us
  other arithmetic: 18.7 us -> 5.82 us
    dot_general x32 -> x0, matrix products: 133 us -> none  [the longest x1 31.5 us: shards(): jnp.einsum('hbk,bhe->khe', back_scores, queries, preferred_element_type=F...]
    pallas_call x1, Pallas kernels: 101 us -> 221 us  [train(): pl.pallas_call(kernel, out_shape=tuple(outputs.values()), in_specs=[pl.Bl...]
    psum x2 -> x0, waiting for transfers between devices: 54.2 us -> none  [the longest x1 27.1 us: shards(): mlp = lax.psum(product(active, down_half).astype(HALF), 'heads')]
    all_gather x2 -> x0, waiting for transfers between devices: 36.9 us -> none  [gather(): return lax.all_gather(rows, 'heads', axis=axis, tiled=True)]
    unnamed x176 -> x41, local copies, waits for them, and re-layouts: 33.3 us -> 8.18 us
    psum x1 -> x0, blocking collectives: 22.2 us -> none  [shards(): query_count = lax.psum(jnp.sum(mask_rows), 'tables')]
    all_gather x2 -> x0, blocking collectives: 14.4 us -> none  [gather(): return lax.all_gather(rows, 'heads', axis=axis, tiled=True)]
    reduce_sum x12 -> x0, other arithmetic: 13.4 us -> none  [the longest x4 6.42 us: normalize(): center = hidden - jnp.mean(hidden, axis=-1, keepdims=True)]
  transfers between devices with their start and end apart: 4 -> 0, of which waited for: 4 -> 0; matrix products, arithmetic and copies ran while one was open for 3% -> 0% of each run, Pallas kernels for 0% -> 0%
where the time goes in v3:
time: 263 us; the launch traced here: 259 us
  Pallas kernels  242 us (92%)
  local copies, waits for them, and re-layouts  9.21 us (4%)
  other arithmetic  5.82 us (2%)
    pallas_call x1, Pallas kernels, train(): pl.pallas_call(kernel, out_shape=tuple(outputs.values()), in_specs=[pl.Bl...  221 us
    pallas_call x1, Pallas kernels, adam_all(): pl.pallas_call(lambda *refs: adam_kernel(refs), grid=(steps,), in_specs=[...  21.3 us
    unnamed x41, local copies, waits for them, and re-layouts  8.18 us

profile of v3, /device:TPU:0, one launch (start us, length us, event | category | flops | bytes accessed | tf_op | source)
XLA Modules:
  0.0 259.2 jit_solution(9495504409424781575)
XLA Ops:
  0.7 0.0 copy-start.18
  0.7 2.9 %convert_element_type.14.refs_11_ = bf16[768,768]{1,0:T(8,128)(2,1)} convert(f32[768,768]{1,0:T(8,128)} %refs_13_.1) | non-fusion elementwise | flops 589824 | bytes 3538944 | tf_op jit(solution)/shard_map/convert_element_type | solution.py:854
  3.6 0.0 copy-done.18
  3.6 0.0 copy-start
  3.6 0.0 copy-start.1
  3.6 1.1 convert_element_type.15.refs_12_
  4.8 0.8 copy-done
  5.5 0.0 copy-start.19
  5.5 1.0 bitcast_convert_fusion.refs_9_
  6.5 0.0 copy-done.1
  6.5 0.7 convert_element_type.13.refs_10_
  7.3 0.0 copy-done.19
  7.3 0.0 copy-start.2
  7.3 0.0 copy-start.3
  7.3 0.0 copy-start.4
  7.3 0.0 copy-start.8
  7.3 0.0 copy-start.14
  7.3 0.0 copy-start.15
  7.3 0.0 copy-start.16
  7.3 0.8 copy.57
  8.1 0.0 copy-start.9
  8.1 0.0 copy-start.10
  8.8 220.8 %train.1 = (bf16[2304,768]{1,0:T(8,128)(2,1)}, bf16[256,768]{1,0:T(8,128)(2,1)}, f32[8,128]{1,0:T(8,128)}) custom-call(s32[1]{0:T(128)S(6)} %copy.58.refs_0_, bf16[512,100]{1,0:T(8,128)(2,1)} %bitcast.25, bf16[176,100]{1,0:T(8,128)(2,1)} %bitcast.26, s32[1,512]{1,0:T(1,128)} %refs_3_.1, s32[1,176]{1,0:T(1,128)} %refs_4_.1, s32[1,176]{1,0:T(1,128)} %refs_5_.1, ...), custom_call_target="tpu_custom_call" | custom-call | tf_op jit(solution)/shard_map/train/pallas_call | solution.py:716
  229.7 0.0 copy-done.2
  229.7 0.0 copy-done.3
  229.7 0.0 copy-done.4
  229.7 0.0 copy-done.8
  229.7 0.0 copy-done.14
  229.7 0.0 copy-done.15
  229.7 0.0 copy-done.16
  229.7 0.0 copy-done.9
  229.7 0.0 copy-done.10
  229.8 0.0 copy-start.5
  229.8 1.1 copy-done.5
  230.8 0.0 copy-start.6
  230.8 1.1 copy-done.6
  231.9 0.0 copy-start.7
  231.9 1.0 copy-done.7
  232.9 0.0 copy-start.11
  232.9 0.9 copy-done.11
  233.8 0.0 copy-start.12
  233.8 0.9 copy-done.12
  234.7 0.0 copy-start.13
  234.7 0.9 copy-done.13
  235.7 0.0 copy-start.17
  235.7 0.7 copy-done.17
  236.4 21.3 %adam.1 = (f32[100,768]{1,0:T(8,128)}, f32[64,768]{1,0:T(8,128)}, f32[3,768]{1,0:T(4,128)}, f32[3,192,768]{2,1,0:T(8,128)}, f32[192,768]{1,0:T(8,128)}, /*index=...) custom-call(f32[8,128]{1,0:T(8,128)S(1)} %copy-done.17, ...), custom_call_target="tpu_custom_call" | custom-call | tf_op jit(solution)/shard_map/adam/pallas_call | solution.py:793
  257.7 0.5 slice.11
  258.2 0.5 fusion
Async XLA Ops:
  0.7 3.0 %copy-start.18 = (f32[768,768]{1,0:T(8,128)S(1)}, f32[768,768]{1,0:T(8,128)}, u32[]{:S(2)}) copy-start(f32[768,768]{1,0:T(8,128)} %refs_14_.1) | copy-start | bytes 7077892
  3.6 1.9 copy-start
  3.6 2.9 %copy-start.1 = (f32[192,768]{1,0:T(8,128)S(1)}, f32[192,768]{1,0:T(8,128)}, u32[]{:S(2)}) copy-start(f32[192,768]{1,0:T(8,128)} %refs_12_.1) | copy-start | bytes 1769476
  5.5 1.8 copy-start.19
  7.3 222.4 %copy-start.2 = (f32[100,768]{1,0:T(8,128)S(1)}, f32[100,768]{1,0:T(8,128)}, u32[]{:S(2)}) copy-start(f32[100,768]{1,0:T(8,128)} %refs_8_.3) | copy-start | bytes 921604
  7.3 222.4 %copy-start.3 = (f32[64,768]{1,0:T(8,128)S(1)}, f32[64,768]{1,0:T(8,128)}, u32[]{:S(2)}) copy-start(f32[64,768]{1,0:T(8,128)} %refs_9_.1) | copy-start | bytes 589828
  7.3 222.4 %copy-start.4 = (f32[768,64]{0,1:T(8,128)S(1)}, f32[768,64]{0,1:T(8,128)}, u32[]{:S(2)}) copy-start(f32[768,64]{0,1:T(8,128)} %param.43) | copy-start | bytes 589828
  7.3 222.4 %copy-start.8 = (f32[100,768]{1,0:T(8,128)S(1)}, f32[100,768]{1,0:T(8,128)}, u32[]{:S(2)}) copy-start(f32[100,768]{1,0:T(8,128)} %refs_16_.1) | copy-start | bytes 921604
  7.3 222.4 %copy-start.14 = (f32[3,768]{1,0:T(4,128)S(1)}, f32[3,768]{1,0:T(4,128)}, u32[]{:S(2)}) copy-start(f32[3,768]{1,0:T(4,128)} %refs_10_.1) | copy-start | bytes 27652
  7.3 222.4 %copy-start.15 = (f32[3,768]{1,0:T(4,128)S(1)}, f32[3,768]{1,0:T(4,128)}, u32[]{:S(2)}) copy-start(f32[3,768]{1,0:T(4,128)} %refs_18_.1) | copy-start | bytes 27652
  7.3 222.4 %copy-start.16 = (f32[3,768]{1,0:T(4,128)S(1)}, f32[3,768]{1,0:T(4,128)}, u32[]{:S(2)}) copy-start(f32[3,768]{1,0:T(4,128)} %refs_26_.1) | copy-start | bytes 27652
  8.1 221.6 %copy-start.9 = (f32[100,768]{1,0:T(8,128)S(1)}, f32[100,768]{1,0:T(8,128)}, u32[]{:S(2)}) copy-start(f32[100,768]{1,0:T(8,128)} %refs_24_.1) | copy-start | bytes 921604
  8.1 221.6 %copy-start.10 = (f32[64,768]{1,0:T(8,128)S(1)}, f32[64,768]{1,0:T(8,128)}, u32[]{:S(2)}) copy-start(f32[64,768]{1,0:T(8,128)} %refs_17_.1) | copy-start | bytes 589828
  229.8 1.1 copy-start.5
  230.8 1.1 copy-start.6
  231.9 1.0 copy-start.7
  232.9 0.9 copy-start.11
  233.8 0.9 copy-start.12
  234.7 0.9 copy-start.13
  235.7 0.7 copy-start.17
